TPU v7x, 32 devices: a whole 2x2x4 slice. The times are simulated.
32 devices in a mesh: mesh: 8 (over z, y), comp: 4 (over x, core).
Axes of the slice: x: 2, y: 2, z: 4, core: 2. Of those that a mesh axis runs over, the one named last changes fastest.
Arguments:
- a_blocks: bfloat16 [1536, 64, 448], P(('mesh', 'comp')), may hold values from -0.25 to 0.25
- a_columns: int32 [1536, 7], P(('mesh', 'comp')), may hold values from 0 to 71, as said below
- p_blocks: bfloat16 [1536, 64, 192], P(('mesh', 'comp')), may hold values from -0.75 to 0.75
- p_columns: int32 [1536, 3], P(('mesh', 'comp')), may hold values from 0 to 3, all different within a row
- r_blocks: bfloat16 [1536, 64, 192], P(('mesh', 'comp')), may hold values from -0.75 to 0.75
- r_columns: int32 [1536, 3], P(('mesh', 'comp')), may hold values from 0 to 11, as said below
- sent_up: int32 [384], P(('mesh', 'comp')), may hold values from 0 to 47, as said below
- sent_down: int32 [384], P(('mesh', 'comp')), may hold values from 0 to 47, as said below
- vectors: bfloat16 [1536, 128], P(('mesh', 'comp')), may hold values from -2 to 2
- coarse_dest: int32 [128, 1], P(('mesh', 'comp')), may hold values from 0 to 3; in each aligned block of 4 rows (0 to 3, 4 to 7, ...) at most 2 rows name the same one
Outputs:
- coarse_matrix: bfloat16 [256, 64, 1280], P(('mesh', 'comp'))
- coarse_vectors: bfloat16 [256, 128], P(('mesh', 'comp'))
Inputs may be any that keep to these rules, and one draw needn't show every extreme that they name: `a_columns`: each fine row's first column is the row itself (its own local number). A column 48 + i exists only on devices with a device below along mesh, 60 + i only on devices with one above; every listed ghost of an existing neighbour is named by some row. `r_columns`: h is never toward a device missing along mesh. Local row numbers; the 12 entries of one device in sent_up and in sent_down are distinct, and no row is in both lists. `sent_down`: see sent_up. `coarse_dest`: at most 2 of the 4 coarse rows of one home go to one owner comp, and that many do in some home. `p_columns`: the 3 entries of a row are distinct.
All inputs are finite; a program needn't handle non-finite values.
Results may differ from a plain program's by a relative error of at most 0.0049.
Values may be sent and summed in bfloat16 or wider, within the bound.
A program may use at most 128 MiB of HBM per device.

v0:
```python
import jax
import jax.numpy as jnp
from jax import lax
from jax.sharding import PartitionSpec as P


def passed_along(block, axis, distance):
    devices = range(lax.axis_size(axis))
    route = [(i - distance, i) for i in devices if i - distance in devices]
    return lax.ppermute(block, axis, route)


def densify(values, columns, coarse_count):
    count = values.shape[0]
    width = values.shape[1]
    blocks = values.reshape(count, width, columns.shape[1], width)
    onehot = (
        columns[:, :, None] == jnp.arange(coarse_count, dtype=jnp.int32)[None, None, :]
    ).astype(jnp.bfloat16)
    dense = jnp.einsum("rqs,rbqc->rbsc", onehot, blocks, preferred_element_type=jnp.float32)
    return dense.astype(jnp.bfloat16).reshape(count, width, coarse_count * width)


def widen(strip, offset, seg_width):
    return jnp.pad(strip, ((0, 0), (0, 0), ((1 - offset) * seg_width, (1 + offset) * seg_width)))


def on_device(
    a_blocks,
    a_columns,
    p_blocks,
    p_columns,
    r_blocks,
    r_columns,
    sent_up,
    sent_down,
    vectors,
    coarse_dest,
):
    fine_rows = a_blocks.shape[0]
    width = a_blocks.shape[1]
    a_count = a_columns.shape[1]
    r_count = r_columns.shape[1]
    ghosts = sent_up.shape[0]
    coarse_count = coarse_dest.shape[0]
    comp_count = lax.axis_size("comp")
    seg_width = coarse_count * width
    own_dense = densify(p_blocks, p_columns, coarse_count)
    from_lower = passed_along(own_dense[sent_up], "mesh", 1)
    from_upper = passed_along(own_dense[sent_down], "mesh", -1)
    p_table = jnp.concatenate([own_dense, from_lower, from_upper], 0)
    coarse_terms = jnp.zeros((3 * coarse_count, width, 3 * seg_width), jnp.float32)
    vec_terms = jnp.zeros((3 * coarse_count, 2, width), jnp.float32)
    gathered = p_table[a_columns]
    segment = jnp.where(a_columns < fine_rows, 1, jnp.where(a_columns < fine_rows + ghosts, 0, 2))
    chooser = (segment[:, :, None] == jnp.arange(3, dtype=jnp.int32)[None, None, :]).astype(
        jnp.float32
    )
    a_rows = a_blocks.reshape(fine_rows, width, a_count, width)
    product = jnp.einsum("fakb,fkbc->fkac", a_rows, gathered, preferred_element_type=jnp.float32)
    applied = jnp.einsum("fke,fkac->faec", chooser, product, precision=lax.Precision.HIGHEST)
    applied = applied.astype(jnp.bfloat16).reshape(fine_rows, width, 3 * seg_width)
    r_rows = r_blocks.reshape(fine_rows, width, r_count, width)
    vec_rows = vectors.reshape(fine_rows, 2, width)
    for j in range(r_count):
        targets = r_columns[0:fine_rows, j]
        contrib = jnp.einsum(
            "fab,fbx->fax", r_rows[:, :, j, :], applied, preferred_element_type=jnp.float32
        )
        coarse_terms = coarse_terms.at[targets].add(contrib)
        vec_part = jnp.einsum(
            "fab,ftb->fta", r_rows[:, :, j, :], vec_rows, preferred_element_type=jnp.float32
        )
        vec_terms = vec_terms.at[targets].add(vec_part)
    lower_piece = coarse_terms[:coarse_count]
    own_piece = coarse_terms[coarse_count : 2 * coarse_count]
    upper_piece = coarse_terms[2 * coarse_count :]
    from_above, above_vec = passed_along(
        (widen(lower_piece, -1, seg_width), vec_terms[:coarse_count]), "mesh", -1
    )
    from_below, below_vec = passed_along(
        (widen(upper_piece, 1, seg_width), vec_terms[2 * coarse_count :]), "mesh", 1
    )
    total = widen(own_piece, 0, seg_width) + from_above + from_below
    restricted = (vec_terms[coarse_count : 2 * coarse_count] + above_vec + below_vec).reshape(
        coarse_count, 2 * width
    )
    coarse_rows = total.astype(jnp.bfloat16)
    coarse_vec = restricted.astype(jnp.bfloat16)
    owner = coarse_dest[:, 0]
    onehot = (owner[:, None] == jnp.arange(comp_count, dtype=jnp.int32)[None, :]).astype(jnp.int32)
    ranking = jnp.sum((jnp.cumsum(onehot, 0) - onehot) * onehot, 1)
    capacity = max(2, coarse_count // 2)
    selector = (owner[None, None, :] == jnp.arange(comp_count, dtype=jnp.int32)[:, None, None]) & (
        ranking[None, None, :] == jnp.arange(capacity, dtype=jnp.int32)[None, :, None]
    )
    selector = selector.astype(jnp.bfloat16)
    outgoing = jnp.einsum(
        "dks,sax->dkax", selector, coarse_rows, preferred_element_type=jnp.float32
    ).astype(jnp.bfloat16)
    outgoing_vec = jnp.einsum(
        "dks,sx->dkx", selector, coarse_vec, preferred_element_type=jnp.float32
    ).astype(jnp.bfloat16)
    received, received_vec = (
        lax.all_to_all(outgoing, "comp", split_axis=0, concat_axis=0, tiled=True),
        lax.all_to_all(outgoing_vec, "comp", split_axis=0, concat_axis=0, tiled=True),
    )
    coarse_matrix = received.reshape(comp_count * capacity, width, 5 * seg_width)
    coarse_vectors = received_vec.reshape(comp_count * capacity, 2 * width)
    return (coarse_matrix, coarse_vectors)


def solution(mesh):
    placed = (
        P(("mesh", "comp"), None, None),
        P(("mesh", "comp"), None),
        P(("mesh", "comp"), None, None),
        P(("mesh", "comp"), None),
        P(("mesh", "comp"), None, None),
        P(("mesh", "comp"), None),
        P(("mesh", "comp")),
        P(("mesh", "comp")),
        P(("mesh", "comp"), None),
        P(("mesh", "comp"), None),
    )
    return jax.shard_map(
        on_device,
        mesh=mesh,
        in_specs=placed,
        out_specs=(P(("mesh", "comp"), None, None), P(("mesh", "comp"), None)),
        check_vma=False,
    )
```

profile of v0, /device:TPU:9, one launch (start us, length us, event | category | flops | bytes accessed | tf_op | source)
XLA Modules:
  0.0 273.3 jit_solution(1670967818803691337)
XLA Ops:
  0.6 2.9 %copy.42 = bf16[48,64,192]{1,2,0:T(8,128)(2,1)S(1)} copy(bf16[48,64,192]{2,1,0:T(8,128)(2,1)} %param.12) | data formatting | bytes 2359296 | tf_op args[2]
  3.5 0.0 copy-start.10
  3.5 3.6 %copy.43 = bf16[48,64,3,64]{3,2,1,0:T(4,128)(2,1)} copy(bf16[48,64,3,64]{1,3,2,0:T(8,128)(2,1)S(1)} %bitcast.76) | data formatting | bytes 2359296 | tf_op jit(solution)/shard_map/reshape | solution.py:16
  7.1 0.1 copy.41
  7.2 3.7 %convert_bitcast_fusion.1 = bf16[48,64,4,64]{3,2,1,0:T(4,128)(2,1)S(1)} fusion(bf16[48,64,3,64]{3,2,1,0:T(4,128)(2,1)} %copy.43, s32[48,3]{1,0:T(8,128)S(1)} %copy.41), kind=kOutput, calls=%fused_computation.17 | convolution fusion | flops 5505600 | bytes 2753088 | tf_op jit(solution)/shard_map/rqs,rbqc->rbsc/dot_general | solution.py:20
  10.9 0.0 copy-start.11
  10.9 0.0 copy-start.12
  10.9 0.0 copy-start.9
  10.9 3.0 %reshape.82 = bf16[48,64,256]{2,1,0:T(8,128)(2,1)} reshape(bf16[48,64,4,64]{3,2,1,0:T(4,128)(2,1)S(1)} %convert_bitcast_fusion.1) | data formatting | bytes 3145728 | tf_op jit(solution)/shard_map/reshape | solution.py:21
  13.9 2.0 gather_fusion
  15.9 3.1 %collective-permute-start = (bf16[12,64,256]{2,1,0:T(8,128)(2,1)S(1)}, bf16[12,64,256]{2,1,0:T(8,128)(2,1)S(1)}, u32[]{:S(2)}, u32[]{:S(2)}) collective-permute-start(bf16[12,64,256]{2,1,0:T(8,128)(2,1)S(1)} %gather_fusion), channel_id=1, source_target_pairs={{0,4},{4,8},{8,12},{12,16},{16,20},{20,24},{24,28},{1,5},{5,9},{9,... | collective-permute-start | bytes 1179656 | tf_op jit(solution)/shard_map/ppermute | solution.py:10
  19.1 2.7 %gather_fusion.1 = bf16[12,64,256]{2,1,0:T(8,128)(2,1)} fusion(bf16[48,64,256]{2,1,0:T(8,128)(2,1)} %reshape.82, s32[1024]{0:T(1024)S(1)} %pad_clamp_fusion.1), kind=kCustom, calls=%fused_computation.1 | custom fusion | bytes 786480 | tf_op jit(solution)/shard_map/gather | solution.py:50
  21.8 3.0 %collective-permute-start.1 = (bf16[12,64,256]{2,1,0:T(8,128)(2,1)}, bf16[12,64,256]{2,1,0:T(8,128)(2,1)S(1)}, u32[]{:S(2)}, u32[]{:S(2)}) collective-permute-start(bf16[12,64,256]{2,1,0:T(8,128)(2,1)} %gather_fusion.1), channel_id=1, source_target_pairs={{4,0},{8,4},{12,8},{16,12},{20,16},{24,20},{28,24},{5,1},{9,5},{13... | collective-permute-start | bytes 1179656 | tf_op jit(solution)/shard_map/ppermute | solution.py:10
  24.9 2.9 %copy.48 = bf16[48,64,192]{1,2,0:T(8,128)(2,1)S(1)} copy(bf16[48,64,192]{2,1,0:T(8,128)(2,1)} %param.14) | data formatting | bytes 2359296 | tf_op args[4]
  27.8 1.4 reshape.87
  29.2 1.7 fusion.5
  30.9 1.3 fusion.26
  32.2 0.7 copy.44
  32.9 0.9 reshape.107
  33.7 9.1 %reshape.83 = bf16[48,64,7,64]{3,2,1,0:T(8,128)(2,1)} reshape(bf16[48,64,448]{2,1,0:T(8,128)(2,1)} %param.10) | data formatting | bytes 5505024 | tf_op jit(solution)/shard_map/reshape | solution.py:59
  42.8 0.7 copy.46
  43.5 1.7 fusion.6
  45.2 0.0 collective-permute-done
  45.2 0.0 collective-permute-done.1
  45.2 1.7 pad_maximum_fusion
  46.9 10.8 %gather_fusion.2 = bf16[336,64,256]{2,1,0:T(8,128)(2,1)} fusion(bf16[72,64,256]{2,1,0:T(8,128)(2,1)S(1)} %pad_maximum_fusion, s32[1024]{0:T(1024)S(1)} %pad_clamp_fusion), kind=kCustom, calls=%fused_computation.2 | custom fusion | bytes 22021440 | tf_op jit(solution)/shard_map/gather | solution.py:54
  57.7 16.3 %convolution_bitcast_fusion = f32[48,7,64,256]{3,2,1,0:T(8,128)} fusion(bf16[48,7,64,256]{3,2,1,0:T(8,128)(2,1)} %bitcast.69, bf16[48,64,7,64]{3,2,1,0:T(8,128)(2,1)} %reshape.83), kind=kOutput, calls=%fused_computation.11 | convolution fusion | flops 704643072 | bytes 35782656 | tf_op jit(solution)/shard_map/fakb,fkbc->fkac/dot_general | solution.py:60
  74.0 31.4 %convert_bitcast_fusion = bf16[48,64,3,256]{3,2,1,0:T(4,128)(2,1)} fusion(f32[48,7,64,256]{3,2,1,0:T(8,128)} %convolution_bitcast_fusion, s32[48,7]{1,0:T(8,128)S(1)} %copy-done.4), kind=kOutput, calls=%fused_computation.12 | convolution fusion | flops 200541168 | bytes 26740032 | tf_op jit(solution)/shard_map/fke,fkac->faec/dot_general | solution.py:61
  105.4 13.1 %reshape.84 = bf16[48,64,768]{2,1,0:T(8,128)(2,1)} reshape(bf16[48,64,3,256]{3,2,1,0:T(4,128)(2,1)} %convert_bitcast_fusion) | data formatting | bytes 9437184 | tf_op jit(solution)/shard_map/reshape | solution.py:62
  118.5 7.5 %convolution_bitcast_fusion.3 = f32[48,64,768]{2,1,0:T(8,128)} fusion(bf16[48,64,768]{2,1,0:T(8,128)(2,1)} %reshape.84, bf16[48,64,3,64]{1,3,2,0:T(8,128)(2,1)S(1)} %bitcast.73), kind=kOutput, calls=%fused_computation.16 | convolution fusion | flops 301989888 | bytes 14942208 | tf_op jit(solution)/shard_map/fab,fbx->fax/dot_general | solution.py:67
  126.1 5.1 %convolution_bitcast_fusion.2 = f32[48,64,768]{2,1,0:T(8,128)} fusion(bf16[48,64,768]{2,1,0:T(8,128)(2,1)S(1)} %copy-done, bf16[48,64,3,64]{1,3,2,0:T(8,128)(2,1)S(1)} %bitcast.74), kind=kOutput, calls=%fused_computation.15 | convolution fusion | flops 301989888 | bytes 14942208 | tf_op jit(solution)/shard_map/fab,fbx->fax/dot_general | solution.py:67
  131.1 5.1 %convolution_bitcast_fusion.1 = f32[48,64,768]{2,1,0:T(8,128)} fusion(bf16[48,64,768]{2,1,0:T(8,128)(2,1)S(1)} %copy-done, bf16[48,64,3,64]{1,3,2,0:T(8,128)(2,1)S(1)} %bitcast.75), kind=kOutput, calls=%fused_computation.14 | convolution fusion | flops 301989888 | bytes 14942208 | tf_op jit(solution)/shard_map/fab,fbx->fax/dot_general | solution.py:67
  136.3 0.2 broadcast_in_dim.20
  136.5 15.0 %scatter_fusion = f32[12,64,768]{2,1,0:T(8,128)S(1)} fusion(f32[12,64,768]{2,1,0:T(8,128)S(1)} %broadcast_in_dim.20, s32[48]{0:T(128)S(1)} %copy-done.8, f32[48,64,768]{2,1,0:T(8,128)} %convolution_bitcast_fusion.3), kind=kCustom, calls=%fused_computation.3 | custom fusion | flops 2359296 | bytes 28311744 | tf_op jit(solution)/shard_map/scatter-add | solution.py:70
  151.5 14.8 %scatter_fusion.1 = f32[12,64,768]{2,1,0:T(8,128)S(1)} fusion(f32[12,64,768]{2,1,0:T(8,128)S(1)} %scatter_fusion, s32[48]{0:T(128)S(1)} %get-tuple-element.11, f32[48,64,768]{2,1,0:T(8,128)} %convolution_bitcast_fusion.2), kind=kCustom, calls=%fused_computation.4 | custom fusion | flops 2359296 | bytes 28311744 | tf_op jit(solution)/shard_map/scatter-add | solution.py:70
  166.3 14.8 %scatter_fusion.2 = f32[12,64,768]{2,1,0:T(8,128)S(1)} fusion(f32[12,64,768]{2,1,0:T(8,128)S(1)} %scatter_fusion.1, s32[48]{0:T(128)S(1)} %get-tuple-element.9, f32[48,64,768]{2,1,0:T(8,128)} %convolution_bitcast_fusion.1), kind=kCustom, calls=%fused_computation.5 | custom fusion | flops 2359296 | bytes 28311744 | tf_op jit(solution)/shard_map/scatter-add | solution.py:70
  181.1 0.2 fusion.27
  181.3 0.0 copy-start.7
  181.3 1.2 pad.13
  182.5 2.1 collective-permute-start.2
  184.6 1.2 pad.14
  185.8 3.2 %collective-permute-start.3 = (f32[4,64,1280]{2,1,0:T(8,128)}, f32[4,64,1280]{2,1,0:T(8,128)}, u32[]{:S(2)}, u32[]{:S(2)}) collective-permute-start(f32[4,64,1280]{2,1,0:T(8,128)} %pad.14), channel_id=1, source_target_pairs={{0,4},{4,8},{8,12},{12,16},{16,20},{20,24},{24,28},{1,5},{5,9},{9,... | collective-permute-start | bytes 3932168 | tf_op jit(solution)/shard_map/ppermute | solution.py:10
  188.9 1.4 fusion.7
  190.4 0.0 copy-done.5
  190.4 2.2 scatter_fusion.3
  192.7 2.2 scatter_fusion.4
  194.9 2.2 scatter_fusion.5
  197.2 3.0 %collective-permute-start.4 = (f32[4,2,64]{2,1,0:T(2,128)S(1)}, f32[4,2,64]{2,1,0:T(2,128)S(1)}, u32[]{:S(2)}, u32[]{:S(2)}) collective-permute-start(f32[4,2,64]{2,1,0:T(2,128)S(1)} %get-tuple-element.5), channel_id=1, source_target_pairs={{4,0},{8,4},{12,8},{16,12},{20,16},{24,20},{28,24},{5,1},{9,5},{13... | collective-permute-start | bytes 6152 | tf_op jit(solution)/shard_map/ppermute | solution.py:10
  200.2 2.3 collective-permute-start.5
  202.5 0.1 iota_compare_fusion.3
  202.6 0.2 select_reduce_fusion
  202.8 39.1 %collective-permute-done.4 = f32[4,2,64]{2,1,0:T(2,128)S(1)} collective-permute-done((f32[4,2,64]{2,1,0:T(2,128)S(1)}, f32[4,2,64]{2,1,0:T(2,128)S(1)}, u32[]{:S(2)}, u32[]{:S(2)}) %collective-permute-start.4) | collective-permute-done | bytes 2080 | tf_op jit(solution)/shard_map/ppermute | solution.py:10
  241.9 0.7 collective-permute-done.5
  242.6 0.1 reshape.169
  242.7 0.1 convolution_convert_fusion.1
  242.9 0.6 copy.54
  243.4 4.6 %all-to-all-start.1 = ((bf16[4,2,128]{2,1,0:T(2,128)(2,1)}), bf16[4,2,128]{2,1,0:T(2,128)(2,1)S(1)}, u32[]{:S(2)}, u32[]{:S(2)}) async-start(bf16[4,2,128]{2,1,0:T(2,128)(2,1)} %copy.54), calls=%async_computation.1 | async-start | bytes 4096 | tf_op jit(solution)/shard_map/all_to_all | solution.py:106
  248.0 1.5 add_convert_fusion
  249.6 0.8 convolution_convert_fusion
  250.4 1.2 copy.53
  251.6 3.6 %all-to-all-start = ((bf16[4,2,64,1280]{3,2,1,0:T(8,128)(2,1)}), bf16[4,2,64,1280]{3,2,1,0:T(8,128)(2,1)S(1)}, u32[]{:S(2)}, u32[]{:S(2)}) async-start(bf16[4,2,64,1280]{3,2,1,0:T(8,128)(2,1)} %copy.53), calls=%async_computation | async-start | bytes 2621440 | tf_op jit(solution)/shard_map/all_to_all | solution.py:105
  255.2 16.4 %all-to-all-done = bf16[4,2,64,1280]{3,2,1,0:T(8,128)(2,1)S(1)} async-done(((bf16[4,2,64,1280]{3,2,1,0:T(8,128)(2,1)}), bf16[4,2,64,1280]{3,2,1,0:T(8,128)(2,1)S(1)}, u32[]{:S(2)}, u32[]{:S(2)}) %all-to-all-start) | async-done | bytes 1310752 | tf_op jit(solution)/shard_map/all_to_all | solution.py:105
  271.6 1.1 copy.79
  272.7 0.6 copy.80
  (34 shorter events, 0.1 us)
Async XLA Ops:
  3.5 3.6 %copy-start.10 = (s32[48,3]{0,1:T(4,128)S(1)}, s32[48,3]{0,1:T(4,128)}, u32[]{:S(2)}) copy-start(s32[48,3]{0,1:T(4,128)} %param.13) | copy-start | bytes 1732
  10.9 3.0 %copy-start.11 = (s32[12]{0:T(128)S(1)}, s32[12]{0:T(128)}, u32[]{:S(2)}) copy-start(s32[12]{0:T(128)} %param.16) | copy-start | bytes 148
  10.9 8.2 %copy-start.12 = (s32[12]{0:T(128)S(1)}, s32[12]{0:T(128)}, u32[]{:S(2)}) copy-start(s32[12]{0:T(128)} %param.17) | copy-start | bytes 148
  10.9 14.0 %copy-start.9 = (s32[48,7]{0,1:T(8,128)S(1)}, s32[48,7]{0,1:T(8,128)}, u32[]{:S(2)}) copy-start(s32[48,7]{0,1:T(8,128)} %param.11) | copy-start | bytes 4036
  15.9 29.3 %collective-permute-start = (bf16[12,64,256]{2,1,0:T(8,128)(2,1)S(1)}, bf16[12,64,256]{2,1,0:T(8,128)(2,1)S(1)}, u32[]{:S(2)}, u32[]{:S(2)}) collective-permute-start(bf16[12,64,256]{2,1,0:T(8,128)(2,1)S(1)} %gather_fusion), channel_id=1, source_target_pairs={{0,4},{4,8},{8,12},{12,16},{16,20},{20,24},{24,28},{1,5},{5,9},{9,... | collective-permute-start | bytes 1179656 | tf_op jit(solution)/shard_map/ppermute | solution.py:10
  21.8 23.4 %collective-permute-start.1 = (bf16[12,64,256]{2,1,0:T(8,128)(2,1)}, bf16[12,64,256]{2,1,0:T(8,128)(2,1)S(1)}, u32[]{:S(2)}, u32[]{:S(2)}) collective-permute-start(bf16[12,64,256]{2,1,0:T(8,128)(2,1)} %gather_fusion.1), channel_id=1, source_target_pairs={{4,0},{8,4},{12,8},{16,12},{20,16},{24,20},{28,24},{5,1},{9,5},{13... | collective-permute-start | bytes 1179656 | tf_op jit(solution)/shard_map/ppermute | solution.py:10
  27.8 15.8 %copy-start.1 = (bf16[48,64,192]{1,2,0:T(8,128)(2,1)}, bf16[48,64,192]{1,2,0:T(8,128)(2,1)S(1)}, u32[]{:S(2)}) copy-start(bf16[48,64,192]{1,2,0:T(8,128)(2,1)S(1)} %copy.48) | copy-start | bytes 3538948
  57.7 16.3 %copy-start.4 = (s32[48,7]{1,0:T(8,128)S(1)}, s32[48,7]{1,0:T(8,128)}, u32[]{:S(2)}) copy-start(s32[48,7]{1,0:T(8,128)} %copy.46) | copy-start | bytes 4036
  105.4 13.1 %copy-start.2 = (bf16[48,64,192]{1,2,0:T(8,128)(2,1)S(1)}, bf16[48,64,192]{1,2,0:T(8,128)(2,1)}, u32[]{:S(2)}) copy-start(bf16[48,64,192]{1,2,0:T(8,128)(2,1)} %copy-done.1) | copy-start | bytes 3538948
  118.5 7.5 %copy-start = (bf16[48,64,768]{2,1,0:T(8,128)(2,1)S(1)}, bf16[48,64,768]{2,1,0:T(8,128)(2,1)}, u32[]{:S(2)}) copy-start(bf16[48,64,768]{2,1,0:T(8,128)(2,1)} %reshape.84) | copy-start | bytes 14155780
  131.1 5.4 %copy-start.8 = (s32[48]{0:T(128)S(1)}, s32[48]{0:T(128)}, u32[]{:S(2)}) copy-start(s32[48]{0:T(128)} %get-tuple-element.10) | copy-start | bytes 580
  181.3 7.6 %copy-start.3 = (bf16[48,2,64]{2,1,0:T(2,128)(2,1)S(1)}, bf16[48,2,64]{2,1,0:T(2,128)(2,1)}, u32[]{:S(2)}) copy-start(bf16[48,2,64]{2,1,0:T(2,128)(2,1)} %reshape.87) | copy-start | bytes 36868
  181.3 9.1 %copy-start.5 = (f32[48,2,64]{2,1,0:T(2,128)S(1)}, f32[48,2,64]{2,1,0:T(2,128)}, u32[]{:S(2)}) copy-start(f32[48,2,64]{2,1,0:T(2,128)} %fusion.5) | copy-start | bytes 73732
  181.3 11.3 %copy-start.6 = (f32[48,2,64]{2,1,0:T(2,128)S(1)}, f32[48,2,64]{2,1,0:T(2,128)}, u32[]{:S(2)}) copy-start(f32[48,2,64]{2,1,0:T(2,128)} %fusion.6) | copy-start | bytes 73732
  181.3 21.1 %copy-start.7 = (s32[4,1]{0,1:T(1,128)S(1)}, s32[4,1]{0,1:T(1,128)}, u32[]{:S(2)}) copy-start(s32[4,1]{0,1:T(1,128)} %param.19) | copy-start | bytes 52
  182.5 65.6 %collective-permute-start.2 = (f32[4,64,1280]{2,1,0:T(8,128)}, f32[4,64,1280]{2,1,0:T(8,128)S(1)}, u32[]{:S(2)}, u32[]{:S(2)}) collective-permute-start(f32[4,64,1280]{2,1,0:T(8,128)} %pad.13), channel_id=1, source_target_pairs={{4,0},{8,4},{12,8},{16,12},{20,16},{24,20},{28,24},{5,1},{9,5},{13... | collective-permute-start | bytes 3932168 | tf_op jit(solution)/shard_map/ppermute | solution.py:10
  185.8 62.3 %collective-permute-start.3 = (f32[4,64,1280]{2,1,0:T(8,128)}, f32[4,64,1280]{2,1,0:T(8,128)}, u32[]{:S(2)}, u32[]{:S(2)}) collective-permute-start(f32[4,64,1280]{2,1,0:T(8,128)} %pad.14), channel_id=1, source_target_pairs={{0,4},{4,8},{8,12},{12,16},{16,20},{20,24},{24,28},{1,5},{5,9},{9,... | collective-permute-start | bytes 3932168 | tf_op jit(solution)/shard_map/ppermute | solution.py:10
  197.2 44.7 %collective-permute-start.4 = (f32[4,2,64]{2,1,0:T(2,128)S(1)}, f32[4,2,64]{2,1,0:T(2,128)S(1)}, u32[]{:S(2)}, u32[]{:S(2)}) collective-permute-start(f32[4,2,64]{2,1,0:T(2,128)S(1)} %get-tuple-element.5), channel_id=1, source_target_pairs={{4,0},{8,4},{12,8},{16,12},{20,16},{24,20},{28,24},{5,1},{9,5},{13... | collective-permute-start | bytes 6152 | tf_op jit(solution)/shard_map/ppermute | solution.py:10
  200.2 42.4 %collective-permute-start.5 = (f32[4,2,64]{2,1,0:T(2,128)S(1)}, f32[4,2,64]{2,1,0:T(2,128)S(1)}, u32[]{:S(2)}, u32[]{:S(2)}) collective-permute-start(f32[4,2,64]{2,1,0:T(2,128)S(1)} %get-tuple-element.6), channel_id=1, source_target_pairs={{0,4},{4,8},{8,12},{12,16},{16,20},{20,24},{24,28},{1,5},{5,9},{9,... | collective-permute-start | bytes 6152 | tf_op jit(solution)/shard_map/ppermute | solution.py:10
  243.4 8.2 %all-to-all-start.1 = ((bf16[4,2,128]{2,1,0:T(2,128)(2,1)}), bf16[4,2,128]{2,1,0:T(2,128)(2,1)S(1)}, u32[]{:S(2)}, u32[]{:S(2)}) async-start(bf16[4,2,128]{2,1,0:T(2,128)(2,1)} %copy.54), calls=%async_computation.1 | async-start | bytes 4096 | tf_op jit(solution)/shard_map/all_to_all | solution.py:106
  251.6 20.0 %all-to-all-start = ((bf16[4,2,64,1280]{3,2,1,0:T(8,128)(2,1)}), bf16[4,2,64,1280]{3,2,1,0:T(8,128)(2,1)S(1)}, u32[]{:S(2)}, u32[]{:S(2)}) async-start(bf16[4,2,64,1280]{3,2,1,0:T(8,128)(2,1)} %copy.53), calls=%async_computation | async-start | bytes 2621440 | tf_op jit(solution)/shard_map/all_to_all | solution.py:105
where the time goes:
time: 276 us; the launch traced here: 273 us
  matrix products  74.8 us (27%)
  local copies, waits for them, and re-layouts  60.1 us (22%)
  waiting for transfers between devices  56.3 us (20%)
  other arithmetic  56.2 us (20%)
  starting transfers between devices  24.9 us (9%)
    scatter-add x3, other arithmetic, on_device(): coarse_terms = coarse_terms.at[targets].add(contrib)  44.6 us
    ppermute x6, waiting for transfers between devices, passed_along(): return lax.ppermute(block, axis, route)  39.9 us
    dot_general x1, matrix products, on_device(): jnp.einsum('fke,fkac->faec', chooser, product, precision=lax.Precision.HI...  31.4 us
    dot_general x3, matrix products, on_device(): jnp.einsum('fab,fbx->fax', r_rows[:, :, j, :], applied, preferred_element...  17.7 us
    ppermute x6, starting transfers between devices, passed_along(): return lax.ppermute(block, axis, route)  16.7 us
    all_to_all x1, waiting for transfers between devices, on_device(): lax.all_to_all(outgoing, 'comp', split_axis=0, concat_axis=0, tiled=True)  16.4 us
    dot_general x1, matrix products, on_device(): jnp.einsum('fakb,fkbc->fkac', a_rows, gathered, preferred_element_type=jn...  16.3 us
    reshape x1, local copies, waits for them, and re-layouts, on_device(): applied.astype(jnp.bfloat16).reshape(fine_rows, width, 3 * seg_width)  13.1 us
  transfers between devices with their start and end apart: 8, of which 3 were waited for; matrix products, arithmetic and copies ran while one was open for 14% of the time, Pallas kernels for 0%

commit v1 on v0

v1 whole, which is shorter than its diff:
```python
import functools

import jax
import jax.numpy as jnp
from jax import lax
from jax.experimental import pallas as pl
from jax.experimental.pallas import tpu as pltpu
from jax.sharding import PartitionSpec as P

MESH = pl.DeviceIdType.MESH
F32 = jnp.float32
BF16 = jnp.bfloat16
UNROLL = 4


def kernel(
    sizes,
    a_cols,
    p_cols,
    r_cols,
    up_rows,
    down_rows,
    dest,
    a_ref,
    p_ref,
    r_ref,
    vec_ref,
    out_ref,
    out_vec,
    eye,
    own,
    ghost,
    ghost_send,
    rd,
    appl,
    part_send,
    part_recv,
    own_part,
    rows,
    slots,
    vec_f32,
    vec_t,
    vpart_send,
    vpart_recv,
    vrows,
    vslots,
    vslots_recv,
    ghost_sems,
    part_sems,
    vpart_sems,
    slot_sems,
    local_sems,
    vslot_sems,
):
    mesh_count, comp_count, nf, width, ka, kp, kr, gh, nc, cap = sizes
    seg = nc * width
    m = lax.axis_index("mesh")
    c = lax.axis_index("comp")
    has_below = m > 0
    has_above = m < mesh_count - 1

    def along(step):
        return (m + step, c)

    def peer(r):
        return (m, lax.rem(c + r, comp_count))

    ghost[...] = jnp.zeros_like(ghost)
    part_recv[...] = jnp.zeros_like(part_recv)
    vpart_recv[...] = jnp.zeros_like(vpart_recv)

    barrier = pltpu.get_barrier_semaphore()
    for r in range(1, comp_count):
        pl.semaphore_signal(barrier, inc=1, device_id=peer(r), device_id_type=MESH)

    @pl.when(has_above)
    def _():
        pl.semaphore_signal(barrier, inc=1, device_id=along(1), device_id_type=MESH)

    @pl.when(has_below)
    def _():
        pl.semaphore_signal(barrier, inc=1, device_id=along(-1), device_id_type=MESH)

    lane = lax.broadcasted_iota(jnp.int32, (width, seg), 1)
    sub = lax.broadcasted_iota(jnp.int32, (width, seg), 0)
    eye[...] = jnp.where((lane & (width - 1)) == sub, 1.0, 0.0).astype(BF16)
    seg_lane = lax.broadcasted_iota(jnp.int32, (1, seg), 1)

    def dense_row(f):
        parts = []
        for q in range(kp):
            start = p_cols[f, q] * width
            hit = (seg_lane >= start) & (seg_lane < start + width)
            parts.append(eye[...] * jnp.where(hit, 1.0, 0.0).astype(BF16))
        spread = jnp.concatenate(parts, axis=0)
        return jnp.dot(p_ref[f], spread, preferred_element_type=F32).astype(BF16)

    def fill_ghosts(listed, at):
        def body(i, carry):
            for t in range(UNROLL):
                g = i * UNROLL + t
                ghost_send[at + g] = dense_row(listed[g])
            return carry

        lax.fori_loop(0, gh // UNROLL, body, 0)

    ghost_up = pltpu.make_async_remote_copy(
        src_ref=ghost_send.at[pl.ds(0, gh)],
        dst_ref=ghost.at[pl.ds(0, gh)],
        send_sem=ghost_sems.at[0],
        recv_sem=ghost_sems.at[1],
        device_id=along(1),
        device_id_type=MESH,
    )
    ghost_down = pltpu.make_async_remote_copy(
        src_ref=ghost_send.at[pl.ds(gh, gh)],
        dst_ref=ghost.at[pl.ds(gh, gh)],
        send_sem=ghost_sems.at[2],
        recv_sem=ghost_sems.at[3],
        device_id=along(-1),
        device_id_type=MESH,
    )
    fill_ghosts(up_rows, 0)
    pl.semaphore_wait(
        barrier,
        comp_count - 1 + jnp.where(has_below, 1, 0) + jnp.where(has_above, 1, 0),
    )

    @pl.when(has_above)
    def _():
        ghost_up.start()

    fill_ghosts(down_rows, gh)

    @pl.when(has_below)
    def _():
        ghost_down.start()

    def own_body(i, carry):
        for t in range(UNROLL):
            f = i * UNROLL + t
            own[f] = dense_row(f)
        return carry

    lax.fori_loop(0, nf // UNROLL, own_body, 0)

    vec_f32[...] = vec_ref[...].astype(F32)
    vec_t[...] = jnp.zeros_like(vec_t)
    pair_lane = lax.broadcasted_iota(jnp.int32, (1, 2 * width), 1)
    first_half = pair_lane < width

    def rd_body(i, carry):
        f = i * 2
        at = pl.ds(pl.multiple_of(i * 2 * width, 2 * width), 2 * width)
        even = r_ref[f]
        odd = r_ref[f + 1]
        blocks = []
        named = []
        for j in range(kr):
            cut = slice(j * width, (j + 1) * width)
            blocks.append(jnp.concatenate([even[:, cut], odd[:, cut]], axis=1))
            named.append(jnp.where(first_half, r_cols[f, j], r_cols[f + 1, j]))
        for target in range(3 * nc):
            total = None
            for j in range(kr):
                hit = jnp.where(named[j] == target, 1.0, 0.0).astype(BF16)
                term = blocks[j] * hit
                total = term if total is None else total + term
            rd[target * width : (target + 1) * width, at] = total
        v0 = vec_f32[pl.ds(f, 1), :]
        v1 = vec_f32[pl.ds(f + 1, 1), :]
        vec_t[0:1, at] = jnp.where(first_half, v0, pltpu.roll(v1, width, 1))
        vec_t[1:2, at] = jnp.where(first_half, pltpu.roll(v0, width, 1), v1)
        return carry

    lax.fori_loop(0, nf // 2, rd_body, 0)

    vec_part = lax.dot_general(
        vec_t[...].astype(BF16),
        rd[...],
        (((1,), (1,)), ((), ())),
        preferred_element_type=F32,
    )
    vpart_send[0] = vec_part[:, 0:seg]
    vpart_send[1] = vec_part[:, 2 * seg : 3 * seg]
    vec_own = vec_part[:, seg : 2 * seg]

    def vpart_copy(way):
        return pltpu.make_async_remote_copy(
            src_ref=vpart_send.at[way],
            dst_ref=vpart_recv.at[way],
            send_sem=vpart_sems.at[way, 0],
            recv_sem=vpart_sems.at[way, 1],
            device_id=along(2 * way - 1),
            device_id_type=MESH,
        )

    def part_copy(way, e):
        return pltpu.make_async_remote_copy(
            src_ref=part_send.at[way, e],
            dst_ref=part_recv.at[way, e],
            send_sem=part_sems.at[way, e, 0],
            recv_sem=part_sems.at[way, e, 1],
            device_id=along(2 * way - 1),
            device_id_type=MESH,
        )

    sends_to = (has_below, has_above)
    gets_from = (has_above, has_below)

    def start(copy, way):
        @pl.when(sends_to[way])
        def _():
            copy.start()

    def wait_recv(copy, way):
        @pl.when(gets_from[way])
        def _():
            copy.wait_recv()

    def wait_send(copy, way):
        @pl.when(sends_to[way])
        def _():
            copy.wait_send()

    for way in range(2):
        start(vpart_copy(way), way)

    a_lane = lax.broadcasted_iota(jnp.int32, (1, ka * width), 1)

    def columns_of(f):
        cols = [a_cols[f, k] for k in range(ka)]
        row = jnp.where(a_lane < width, cols[0], cols[1])
        for k in range(2, ka):
            row = jnp.where(a_lane >= k * width, cols[k], row)
        return cols, row

    def at_row(f):
        return pl.ds(pl.multiple_of(f * width, width), width)

    def near_body(i, carry):
        for t in range(UNROLL):
            f = i * UNROLL + t
            cols, row = columns_of(f)
            keep = jnp.where(row < nf, 1.0, 0.0).astype(BF16)
            table = jnp.concatenate([own[jnp.where(x < nf, x, 0)] for x in cols], axis=0)
            product = jnp.dot(a_ref[f] * keep, table, preferred_element_type=F32)
            appl[1, at_row(f), :] = product.astype(BF16)
        return carry

    lax.fori_loop(0, nf // UNROLL, near_body, 0)

    def restricted(side, e):
        return jnp.dot(
            rd[side * seg : (side + 1) * seg, :], appl[e], preferred_element_type=F32
        )

    def send_part(way, e):
        part_send[way, e] = restricted(2 * way, e).astype(BF16)
        start(part_copy(way, e), way)

    send_part(0, 1)
    send_part(1, 1)
    own_part[1] = restricted(1, 1)

    @pl.when(has_below)
    def _():
        ghost_up.wait_recv()

    @pl.when(has_above)
    def _():
        ghost_down.wait_recv()

    def far_body(i, carry):
        for t in range(UNROLL):
            f = i * UNROLL + t
            cols, row = columns_of(f)
            a_row = a_ref[f]
            low = jnp.where((row >= nf) & (row < nf + gh), 1.0, 0.0).astype(BF16)
            high = jnp.where(row >= nf + gh, 1.0, 0.0).astype(BF16)
            both = jnp.concatenate([a_row * low, a_row * high], axis=0)
            table = jnp.concatenate([ghost[jnp.where(x < nf, 0, x - nf)] for x in cols], axis=0)
            product = jnp.dot(both, table, preferred_element_type=F32).astype(BF16)
            appl[0, at_row(f), :] = product[:width]
            appl[2, at_row(f), :] = product[width:]
        return carry

    lax.fori_loop(0, nf // UNROLL, far_body, 0)
    send_part(1, 0)
    send_part(0, 2)
    send_part(1, 2)
    send_part(0, 0)
    own_part[0] = restricted(1, 0)
    own_part[2] = restricted(1, 2)

    owners = [dest[s, 0] for s in range(nc)]
    ranks = []
    for s in range(nc):
        rank = jnp.int32(0)
        for before in range(s):
            rank = rank + jnp.where(owners[before] == owners[s], 1, 0)
        ranks.append(rank)
    sources = []
    for r in range(comp_count):
        to = lax.rem(c + r, comp_count)
        for k in range(cap):
            source = jnp.int32(nc)
            for s in range(nc):
                source = jnp.where((owners[s] == to) & (ranks[s] == k), s, source)
            sources.append(source)

    own_rows = pl.ds(c * cap, cap)

    def slot_copy(u, r):
        return pltpu.make_async_remote_copy(
            src_ref=slots.at[u, r],
            dst_ref=out_ref.at[own_rows, :, pl.ds(u * seg, seg)],
            send_sem=slot_sems.at[u, r - 1, 0],
            recv_sem=slot_sems.at[u, r - 1, 1],
            device_id=peer(r),
            device_id_type=MESH,
        )

    def local_copy(u):
        return pltpu.make_async_copy(
            slots.at[u, 0], out_ref.at[own_rows, :, pl.ds(u * seg, seg)], local_sems.at[u]
        )

    def finish(u):
        total = None
        if 1 <= u <= 3:
            total = own_part[u - 1]
        if u >= 2:
            term = part_recv[0, u - 2].astype(F32)
            total = term if total is None else total + term
        if u <= 2:
            term = part_recv[1, u].astype(F32)
            total = term if total is None else total + term
        rounded = total.astype(BF16)
        for s in range(nc):
            rows[u, s] = rounded[s * width : (s + 1) * width]
        rows[u, nc] = jnp.zeros((width, seg), BF16)
        for r in range(1, comp_count):
            for k in range(cap):
                slots[u, r, k] = rows[u, sources[r * cap + k]]
            slot_copy(u, r).start()
        for k in range(cap):
            slots[u, 0, k] = rows[u, sources[k]]
        local_copy(u).start()

    for way in range(2):
        wait_recv(vpart_copy(way), way)
    vec_total = vec_own + vpart_recv[0] + vpart_recv[1]
    vrows[...] = jnp.zeros_like(vrows)
    for s in range(nc):
        cut = slice(s * width, (s + 1) * width)
        both = jnp.concatenate([vec_total[0:1, cut], vec_total[1:2, cut]], axis=1)
        vrows[s, 0:1, :] = both
    for r in range(comp_count):
        picked = [vrows[sources[r * cap + k]] for k in range(cap)]
        for k in range(cap):
            vslots[r, k] = picked[k]

    def vslot_copy(r):
        return pltpu.make_async_remote_copy(
            src_ref=vslots.at[r],
            dst_ref=vslots_recv.at[r],
            send_sem=vslot_sems.at[r - 1, 0],
            recv_sem=vslot_sems.at[r - 1, 1],
            device_id=peer(r),
            device_id_type=MESH,
        )

    for r in range(1, comp_count):
        vslot_copy(r).start()

    wait_recv(part_copy(1, 1), 1)
    finish(1)
    wait_recv(part_copy(0, 1), 0)
    finish(3)
    wait_recv(part_copy(1, 0), 1)
    finish(0)
    wait_recv(part_copy(0, 2), 0)
    finish(4)
    wait_recv(part_copy(1, 2), 1)
    wait_recv(part_copy(0, 0), 0)
    finish(2)

    vslots_recv[0] = vslots[0]
    for r in range(1, comp_count):
        vslot_copy(r).wait_recv()
    for x in range(comp_count):
        for k in range(cap):
            row = jnp.zeros((1, 2 * width), F32)
            for r in range(comp_count):
                from_x = lax.rem(c + comp_count - r, comp_count) == x
                row = row + jnp.where(from_x, 1.0, 0.0) * vslots_recv[r, k, 0:1, :]
            out_vec[x * cap + k : x * cap + k + 1, :] = row

    for u in range(5):
        for r in range(1, comp_count):
            slot_copy(u, r).wait_recv()
        local_copy(u).wait()
    for r in range(1, comp_count):
        vslot_copy(r).wait_send()
        for u in range(5):
            slot_copy(u, r).wait_send()
    for way in range(2):
        wait_send(vpart_copy(way), way)
        for e in range(3):
            wait_send(part_copy(way, e), way)

    @pl.when(has_above)
    def _():
        ghost_up.wait_send()

    @pl.when(has_below)
    def _():
        ghost_down.wait_send()


def on_device(
    mesh_count,
    comp_count,
    a_blocks,
    a_columns,
    p_blocks,
    p_columns,
    r_blocks,
    r_columns,
    sent_up,
    sent_down,
    vectors,
    coarse_dest,
):
    nf, width = a_blocks.shape[:2]
    ka, kp, kr = a_columns.shape[1], p_columns.shape[1], r_columns.shape[1]
    gh, nc = sent_up.shape[0], coarse_dest.shape[0]
    cap = max(2, nc // 2)
    seg = nc * width
    sizes = (mesh_count, comp_count, nf, width, ka, kp, kr, gh, nc, cap)
    smem = pl.BlockSpec(memory_space=pltpu.SMEM)
    vmem = pl.BlockSpec(memory_space=pltpu.VMEM)
    matrix, vecs = pl.pallas_call(
        functools.partial(kernel, sizes),
        out_shape=(
            jax.ShapeDtypeStruct((comp_count * cap, width, 5 * seg), BF16),
            jax.ShapeDtypeStruct((comp_count * cap, 2 * width), F32),
        ),
        in_specs=[smem] * 6 + [vmem] * 4,
        out_specs=(pl.BlockSpec(memory_space=pl.ANY), vmem),
        scratch_shapes=[
            pltpu.VMEM((width, seg), BF16),
            pltpu.VMEM((nf, width, seg), BF16),
            pltpu.VMEM((2 * gh, width, seg), BF16),
            pltpu.VMEM((2 * gh, width, seg), BF16),
            pltpu.VMEM((3 * seg, nf * width), BF16),
            pltpu.VMEM((3, nf * width, seg), BF16),
            pltpu.VMEM((2, 3, seg, seg), BF16),
            pltpu.VMEM((2, 3, seg, seg), BF16),
            pltpu.VMEM((3, seg, seg), F32),
            pltpu.VMEM((5, nc + 1, width, seg), BF16),
            pltpu.VMEM((5, comp_count, cap, width, seg), BF16),
            pltpu.VMEM((nf, 2 * width), F32),
            pltpu.VMEM((8, nf * width), F32),
            pltpu.VMEM((2, 8, seg), F32),
            pltpu.VMEM((2, 8, seg), F32),
            pltpu.VMEM((nc + 1, 8, 2 * width), F32),
            pltpu.VMEM((comp_count, cap, 8, 2 * width), F32),
            pltpu.VMEM((comp_count, cap, 8, 2 * width), F32),
            pltpu.SemaphoreType.DMA((4,)),
            pltpu.SemaphoreType.DMA((2, 3, 2)),
            pltpu.SemaphoreType.DMA((2, 2)),
            pltpu.SemaphoreType.DMA((5, comp_count - 1, 2)),
            pltpu.SemaphoreType.DMA((5,)),
            pltpu.SemaphoreType.DMA((comp_count - 1, 2)),
        ],
        compiler_params=pltpu.CompilerParams(
            collective_id=0, has_side_effects=True, vmem_limit_bytes=48 * 1024 * 1024
        ),
    )(
        a_columns,
        p_columns,
        r_columns,
        sent_up,
        sent_down,
        coarse_dest,
        a_blocks,
        p_blocks,
        r_blocks,
        vectors,
    )
    return matrix, vecs.astype(BF16)


def solution(mesh):
    placed = (
        P(("mesh", "comp"), None, None),
        P(("mesh", "comp"), None),
        P(("mesh", "comp"), None, None),
        P(("mesh", "comp"), None),
        P(("mesh", "comp"), None, None),
        P(("mesh", "comp"), None),
        P(("mesh", "comp")),
        P(("mesh", "comp")),
        P(("mesh", "comp"), None),
        P(("mesh", "comp"), None),
    )
    return jax.shard_map(
        functools.partial(on_device, mesh.shape["mesh"], mesh.shape["comp"]),
        mesh=mesh,
        in_specs=placed,
        out_specs=(P(("mesh", "comp"), None, None), P(("mesh", "comp"), None)),
        check_vma=False,
    )
```

time: 276 us -> 61.8 us (0.22)
  matrix products: 74.8 us -> 0 us
  waiting for transfers between devices: 56.3 us -> 0 us
  other arithmetic: 56.2 us -> 0.58 us
  Pallas kernels: 0 us -> 51.2 us
  local copies, waits for them, and re-layouts: 60.1 us -> 8.93 us
  starting transfers between devices: 24.9 us -> 0 us
    dot_general x11 -> x0, matrix products: 74.8 us -> none  [the longest x1 31.4 us: on_device(): jnp.einsum('fke,fkac->faec', chooser, product, precision=lax.Precision.HI...]
    scatter-add x6 -> x0, other arithmetic: 51.3 us -> none  [the longest x3 44.6 us: on_device(): coarse_terms = coarse_terms.at[targets].add(contrib)]
    pallas_call x0 -> x1, Pallas kernels: none -> 51.2 us  [on_device(): pl.pallas_call(functools.partial(kernel, sizes), out_shape=(jax.ShapeDtyp...]
    ppermute x6 -> x0, waiting for transfers between devices: 39.9 us -> none  [passed_along(): return lax.ppermute(block, axis, route)]
    reshape x5 -> x0, local copies, waits for them, and re-layouts: 30.3 us -> none  [the longest x1 13.1 us: on_device(): applied.astype(jnp.bfloat16).reshape(fine_rows, width, 3 * seg_width)]
    ppermute x6 -> x0, starting transfers between devices: 16.7 us -> none  [passed_along(): return lax.ppermute(block, axis, route)]
    all_to_all x2 -> x0, waiting for transfers between devices: 16.4 us -> none  [the longest x1 16.4 us: on_device(): lax.all_to_all(outgoing, 'comp', split_axis=0, concat_axis=0, tiled=True)]
    gather x3 -> x0, local copies, waits for them, and re-layouts: 15.6 us -> none  [the longest x1 10.8 us: on_device(): gathered = p_table[a_columns]]
  transfers between devices with their start and end apart: 8 -> 0, of which waited for: 3 -> 0; matrix products, arithmetic and copies ran while one was open for 14% -> 0% of each run, Pallas kernels for 0% -> 0%
where the time goes in v1:
time: 61.8 us; the launch traced here: 61.4 us
  Pallas kernels  51.2 us (83%)
  local copies, waits for them, and re-layouts  8.93 us (14%)
  between operations  0.65 us (1%)
    pallas_call x1, Pallas kernels, on_device(): pl.pallas_call(functools.partial(kernel, sizes), out_shape=(jax.ShapeDtyp...  51.2 us
    unnamed x15, local copies, waits for them, and re-layouts  8.93 us

profile of v1, /device:TPU:9, one launch (start us, length us, event | category | flops | bytes accessed | tf_op | source)
XLA Modules:
  0.0 61.4 jit_solution(3029587890828666686)
XLA Ops:
  0.6 0.7 %copy.15.dest = s32[4,1]{1,0:T(4,128)S(1)} copy(s32[4,1]{0,1:T(1,128)} %param.19) | data formatting | bytes 32 | tf_op args[9]
  1.4 0.8 %copy.12.a_cols = s32[48,7]{1,0:T(8,128)S(1)} copy(s32[48,7]{0,1:T(8,128)} %param.11) | data formatting | bytes 2688 | tf_op args[1]
  2.1 0.8 %copy.13.p_cols = s32[48,3]{1,0:T(8,128)S(1)} copy(s32[48,3]{0,1:T(4,128)} %param.13) | data formatting | bytes 1152 | tf_op args[3]
  2.9 0.8 %copy.14.r_cols = s32[48,3]{1,0:T(8,128)S(1)} copy(s32[48,3]{0,1:T(4,128)} %param.15) | data formatting | bytes 1152 | tf_op args[5]
  3.7 0.0 copy-start
  3.7 1.4 %copy-done = bf16[48,64,192]{2,1,0:T(8,128)(2,1)S(1)} copy-done((bf16[48,64,192]{2,1,0:T(8,128)(2,1)S(1)}, bf16[48,64,192]{2,1,0:T(8,128)(2,1)}, u32[]{:S(2)}) %copy-start) | copy-done | bytes 1179672
  5.1 0.0 copy-start.1
  5.1 1.4 %copy-done.1 = bf16[48,64,192]{2,1,0:T(8,128)(2,1)S(1)} copy-done((bf16[48,64,192]{2,1,0:T(8,128)(2,1)S(1)}, bf16[48,64,192]{2,1,0:T(8,128)(2,1)}, u32[]{:S(2)}) %copy-start.1) | copy-done | bytes 1179672
  6.5 0.0 copy-start.2
  6.5 0.7 %copy-done.2 = bf16[48,128]{1,0:T(8,128)(2,1)S(1)} copy-done((bf16[48,128]{1,0:T(8,128)(2,1)S(1)}, bf16[48,128]{1,0:T(8,128)(2,1)}, u32[]{:S(2)}) %copy-start.2) | copy-done | bytes 12312
  7.2 0.0 copy-start.3
  7.2 0.7 %copy-done.3 = s32[12]{0:T(128)S(1)} copy-done((s32[12]{0:T(128)S(1)}, s32[12]{0:T(128)}, u32[]{:S(2)}) %copy-start.3) | copy-done | bytes 72
  7.9 0.0 copy-start.4
  7.9 0.7 %copy-done.4 = s32[12]{0:T(128)S(1)} copy-done((s32[12]{0:T(128)S(1)}, s32[12]{0:T(128)}, u32[]{:S(2)}) %copy-start.4) | copy-done | bytes 72
  8.5 51.2 %shard_map.113 = (bf16[8,64,1280]{2,1,0:T(8,128)(2,1)S(1)}, f32[8,128]{1,0:T(8,128)S(1)}) custom-call(s32[48,7]{1,0:T(8,128)S(1)} %copy.12.a_cols, s32[48,3]{1,0:T(8,128)S(1)} %copy.13.p_cols, s32[48,3]{1,0:T(8,128)S(1)} %copy.14.r_cols, s32[12]{0:T(128)S(1)} %copy-done.3, s32[12]{0:T(128)S(1)} %copy-done.4, s32[4,1]{1,0:T(4,128)S(1)} %copy.15.dest, ...), custom_call_target="tpu_custom_call" | custom-call | tf_op jit(solution)/shard_map/pallas_call | solution.py:444
  59.7 0.6 convert_element_type.3
  60.3 1.1 %copy.17 = bf16[8,64,1280]{2,1,0:T(8,128)(2,1)} copy(bf16[8,64,1280]{2,1,0:T(8,128)(2,1)S(1)} %get-tuple-element.8) | data formatting | bytes 2621440
Async XLA Ops:
  3.7 1.4 %copy-start = (bf16[48,64,192]{2,1,0:T(8,128)(2,1)S(1)}, bf16[48,64,192]{2,1,0:T(8,128)(2,1)}, u32[]{:S(2)}) copy-start(bf16[48,64,192]{2,1,0:T(8,128)(2,1)} %p_ref.1) | copy-start | bytes 3538948
  5.1 1.4 %copy-start.1 = (bf16[48,64,192]{2,1,0:T(8,128)(2,1)S(1)}, bf16[48,64,192]{2,1,0:T(8,128)(2,1)}, u32[]{:S(2)}) copy-start(bf16[48,64,192]{2,1,0:T(8,128)(2,1)} %r_ref.1) | copy-start | bytes 3538948
  6.5 0.7 %copy-start.2 = (bf16[48,128]{1,0:T(8,128)(2,1)S(1)}, bf16[48,128]{1,0:T(8,128)(2,1)}, u32[]{:S(2)}) copy-start(bf16[48,128]{1,0:T(8,128)(2,1)} %vec_ref.1) | copy-start | bytes 36868
  7.2 0.7 %copy-start.3 = (s32[12]{0:T(128)S(1)}, s32[12]{0:T(128)}, u32[]{:S(2)}) copy-start(s32[12]{0:T(128)} %up_rows.1) | copy-start | bytes 148
  7.9 0.7 %copy-start.4 = (s32[12]{0:T(128)S(1)}, s32[12]{0:T(128)}, u32[]{:S(2)}) copy-start(s32[12]{0:T(128)} %down_rows.1) | copy-start | bytes 148

commit v2 on v1

--- a/solution.py
+++ b/solution.py
@@ -11,6 +11,7 @@
 F32 = jnp.float32
 BF16 = jnp.bfloat16
 UNROLL = 4
+WIDE = 8
 
 
 def kernel(
@@ -21,13 +22,16 @@
     up_rows,
     down_rows,
     dest,
+    a_hbm,
+    p_hbm,
+    r_hbm,
+    vec_hbm,
+    out_ref,
+    out_vec,
     a_ref,
     p_ref,
     r_ref,
     vec_ref,
-    out_ref,
-    out_vec,
-    eye,
     own,
     ghost,
     ghost_send,
@@ -51,6 +55,7 @@
     slot_sems,
     local_sems,
     vslot_sems,
+    in_sems,
 ):
     mesh_count, comp_count, nf, width, ka, kp, kr, gh, nc, cap = sizes
     seg = nc * width
@@ -65,6 +70,15 @@
     def peer(r):
         return (m, lax.rem(c + r, comp_count))
 
+    inputs = [
+        pltpu.make_async_copy(source, target, in_sems.at[i])
+        for i, (source, target) in enumerate(
+            ((p_hbm, p_ref), (r_hbm, r_ref), (vec_hbm, vec_ref), (a_hbm, a_ref))
+        )
+    ]
+    for copy in inputs:
+        copy.start()
+
     ghost[...] = jnp.zeros_like(ghost)
     part_recv[...] = jnp.zeros_like(part_recv)
     vpart_recv[...] = jnp.zeros_like(vpart_recv)
@@ -81,19 +95,24 @@
     def _():
         pl.semaphore_signal(barrier, inc=1, device_id=along(-1), device_id_type=MESH)
 
-    lane = lax.broadcasted_iota(jnp.int32, (width, seg), 1)
-    sub = lax.broadcasted_iota(jnp.int32, (width, seg), 0)
-    eye[...] = jnp.where((lane & (width - 1)) == sub, 1.0, 0.0).astype(BF16)
-    seg_lane = lax.broadcasted_iota(jnp.int32, (1, seg), 1)
+    pair_lane = lax.broadcasted_iota(jnp.int32, (1, 2 * width), 1)
+    first_half = pair_lane < width
 
     def dense_row(f):
-        parts = []
+        strip = p_ref[f]
+        blocks = []
         for q in range(kp):
-            start = p_cols[f, q] * width
-            hit = (seg_lane >= start) & (seg_lane < start + width)
-            parts.append(eye[...] * jnp.where(hit, 1.0, 0.0).astype(BF16))
-        spread = jnp.concatenate(parts, axis=0)
-        return jnp.dot(p_ref[f], spread, preferred_element_type=F32).astype(BF16)
+            block = strip[:, q * width : (q + 1) * width]
+            blocks.append(jnp.concatenate([block, block], axis=1))
+        tiles = []
+        for s in range(0, nc, 2):
+            here = jnp.where(first_half, s, s + 1)
+            total = None
+            for q in range(kp):
+                term = blocks[q] * jnp.where(here == p_cols[q, f], 1.0, 0.0).astype(BF16)
+                total = term if total is None else total + term
+            tiles.append(total)
+        return jnp.concatenate(tiles, axis=1)
 
     def fill_ghosts(listed, at):
         def body(i, carry):
@@ -120,6 +139,7 @@
         device_id=along(-1),
         device_id_type=MESH,
     )
+    inputs[0].wait()
     fill_ghosts(up_rows, 0)
     pl.semaphore_wait(
         barrier,
@@ -144,11 +164,10 @@
 
     lax.fori_loop(0, nf // UNROLL, own_body, 0)
 
+    inputs[1].wait()
+    inputs[2].wait()
     vec_f32[...] = vec_ref[...].astype(F32)
     vec_t[...] = jnp.zeros_like(vec_t)
-    pair_lane = lax.broadcasted_iota(jnp.int32, (1, 2 * width), 1)
-    first_half = pair_lane < width
-
     def rd_body(i, carry):
         f = i * 2
         at = pl.ds(pl.multiple_of(i * 2 * width, 2 * width), 2 * width)
@@ -159,7 +178,7 @@
         for j in range(kr):
             cut = slice(j * width, (j + 1) * width)
             blocks.append(jnp.concatenate([even[:, cut], odd[:, cut]], axis=1))
-            named.append(jnp.where(first_half, r_cols[f, j], r_cols[f + 1, j]))
+            named.append(jnp.where(first_half, r_cols[j, f], r_cols[j, f + 1]))
         for target in range(3 * nc):
             total = None
             for j in range(kr):
@@ -229,7 +248,7 @@
     a_lane = lax.broadcasted_iota(jnp.int32, (1, ka * width), 1)
 
     def columns_of(f):
-        cols = [a_cols[f, k] for k in range(ka)]
+        cols = [a_cols[k, f] for k in range(ka)]
         row = jnp.where(a_lane < width, cols[0], cols[1])
         for k in range(2, ka):
             row = jnp.where(a_lane >= k * width, cols[k], row)
@@ -239,8 +258,8 @@
         return pl.ds(pl.multiple_of(f * width, width), width)
 
     def near_body(i, carry):
-        for t in range(UNROLL):
-            f = i * UNROLL + t
+        for t in range(WIDE):
+            f = i * WIDE + t
             cols, row = columns_of(f)
             keep = jnp.where(row < nf, 1.0, 0.0).astype(BF16)
             table = jnp.concatenate([own[jnp.where(x < nf, x, 0)] for x in cols], axis=0)
@@ -248,20 +267,18 @@
             appl[1, at_row(f), :] = product.astype(BF16)
         return carry
 
-    lax.fori_loop(0, nf // UNROLL, near_body, 0)
-
-    def restricted(side, e):
-        return jnp.dot(
-            rd[side * seg : (side + 1) * seg, :], appl[e], preferred_element_type=F32
-        )
-
-    def send_part(way, e):
-        part_send[way, e] = restricted(2 * way, e).astype(BF16)
-        start(part_copy(way, e), way)
-
-    send_part(0, 1)
-    send_part(1, 1)
-    own_part[1] = restricted(1, 1)
+    inputs[3].wait()
+    lax.fori_loop(0, nf // WIDE, near_body, 0)
+
+    def restrict(e):
+        terms = jnp.dot(rd[...], appl[e], preferred_element_type=F32)
+        part_send[0, e] = terms[:seg].astype(BF16)
+        own_part[e] = terms[seg : 2 * seg]
+        part_send[1, e] = terms[2 * seg :].astype(BF16)
+
+    restrict(1)
+    for way in range(2):
+        start(part_copy(way, 1), way)
 
     @pl.when(has_below)
     def _():
@@ -272,8 +289,8 @@
         ghost_down.wait_recv()
 
     def far_body(i, carry):
-        for t in range(UNROLL):
-            f = i * UNROLL + t
+        for t in range(WIDE):
+            f = i * WIDE + t
             cols, row = columns_of(f)
             a_row = a_ref[f]
             low = jnp.where((row >= nf) & (row < nf + gh), 1.0, 0.0).astype(BF16)
@@ -285,15 +302,15 @@
             appl[2, at_row(f), :] = product[width:]
         return carry
 
-    lax.fori_loop(0, nf // UNROLL, far_body, 0)
-    send_part(1, 0)
-    send_part(0, 2)
-    send_part(1, 2)
-    send_part(0, 0)
-    own_part[0] = restricted(1, 0)
-    own_part[2] = restricted(1, 2)
-
-    owners = [dest[s, 0] for s in range(nc)]
+    lax.fori_loop(0, nf // WIDE, far_body, 0)
+    restrict(0)
+    start(part_copy(1, 0), 1)
+    restrict(2)
+    start(part_copy(0, 2), 0)
+    start(part_copy(1, 2), 1)
+    start(part_copy(0, 0), 0)
+
+    owners = [dest[s] for s in range(nc)]
     ranks = []
     for s in range(nc):
         rank = jnp.int32(0)
@@ -389,13 +406,15 @@
     vslots_recv[0] = vslots[0]
     for r in range(1, comp_count):
         vslot_copy(r).wait_recv()
+    vec_rows = []
     for x in range(comp_count):
         for k in range(cap):
             row = jnp.zeros((1, 2 * width), F32)
             for r in range(comp_count):
                 from_x = lax.rem(c + comp_count - r, comp_count) == x
                 row = row + jnp.where(from_x, 1.0, 0.0) * vslots_recv[r, k, 0:1, :]
-            out_vec[x * cap + k : x * cap + k + 1, :] = row
+            vec_rows.append(row)
+    out_vec[...] = jnp.concatenate(vec_rows, axis=0).astype(BF16)
 
     for u in range(5):
         for r in range(1, comp_count):
@@ -440,17 +459,21 @@
     seg = nc * width
     sizes = (mesh_count, comp_count, nf, width, ka, kp, kr, gh, nc, cap)
     smem = pl.BlockSpec(memory_space=pltpu.SMEM)
+    hbm = pl.BlockSpec(memory_space=pl.ANY)
     vmem = pl.BlockSpec(memory_space=pltpu.VMEM)
-    matrix, vecs = pl.pallas_call(
+    return pl.pallas_call(
         functools.partial(kernel, sizes),
         out_shape=(
             jax.ShapeDtypeStruct((comp_count * cap, width, 5 * seg), BF16),
-            jax.ShapeDtypeStruct((comp_count * cap, 2 * width), F32),
+            jax.ShapeDtypeStruct((comp_count * cap, 2 * width), BF16),
         ),
-        in_specs=[smem] * 6 + [vmem] * 4,
-        out_specs=(pl.BlockSpec(memory_space=pl.ANY), vmem),
+        in_specs=[smem] * 6 + [hbm] * 4,
+        out_specs=(hbm, vmem),
         scratch_shapes=[
-            pltpu.VMEM((width, seg), BF16),
+            pltpu.VMEM(a_blocks.shape, BF16),
+            pltpu.VMEM(p_blocks.shape, BF16),
+            pltpu.VMEM(r_blocks.shape, BF16),
+            pltpu.VMEM(vectors.shape, BF16),
             pltpu.VMEM((nf, width, seg), BF16),
             pltpu.VMEM((2 * gh, width, seg), BF16),
             pltpu.VMEM((2 * gh, width, seg), BF16),
@@ -474,23 +497,23 @@
             pltpu.SemaphoreType.DMA((5, comp_count - 1, 2)),
             pltpu.SemaphoreType.DMA((5,)),
             pltpu.SemaphoreType.DMA((comp_count - 1, 2)),
+            pltpu.SemaphoreType.DMA((4,)),
         ],
         compiler_params=pltpu.CompilerParams(
-            collective_id=0, has_side_effects=True, vmem_limit_bytes=48 * 1024 * 1024
+            collective_id=0, has_side_effects=True, vmem_limit_bytes=60 * 1024 * 1024
         ),
     )(
-        a_columns,
-        p_columns,
-        r_columns,
+        a_columns.T,
+        p_columns.T,
+        r_columns.T,
         sent_up,
         sent_down,
-        coarse_dest,
+        coarse_dest.reshape(nc),
         a_blocks,
         p_blocks,
         r_blocks,
         vectors,
     )
-    return matrix, vecs.astype(BF16)
 
 
 def solution(mesh):

time: 61.8 us -> 54.5 us (0.88)
  local copies, waits for them, and re-layouts: 8.93 us -> 3.05 us
    unnamed x15 -> x4, local copies, waits for them, and re-layouts: 8.93 us -> 3.05 us
    pallas_call x1, Pallas kernels: 51.2 us -> 50.6 us  [on_device(): pl.pallas_call(functools.partial(kernel, sizes), out_shape=(jax.ShapeDtyp...]
where the time goes in v2:
time: 54.5 us; the launch traced here: 54.3 us
  Pallas kernels  50.6 us (93%)
  local copies, waits for them, and re-layouts  3.05 us (6%)
  between operations  0.65 us (1%)
    pallas_call x1, Pallas kernels, on_device(): pl.pallas_call(functools.partial(kernel, sizes), out_shape=(jax.ShapeDtyp...  50.6 us
    unnamed x4, local copies, waits for them, and re-layouts  3.05 us

profile of v2, /device:TPU:9, one launch (start us, length us, event | category | flops | bytes accessed | tf_op | source)
XLA Modules:
  0.0 54.3 jit_solution(6113827884719421912)
XLA Ops:
  0.6 50.6 %shard_map.113 = (bf16[8,64,1280]{2,1,0:T(8,128)(2,1)}, bf16[8,128]{1,0:T(8,128)(2,1)}) custom-call(s32[7,48]{1,0:T(8,128)} %bitcast.4, s32[3,48]{1,0:T(4,128)} %bitcast.5, s32[3,48]{1,0:T(4,128)} %bitcast.6, s32[12]{0:T(128)} %up_rows.1, s32[12]{0:T(128)} %down_rows.1, s32[4]{0:T(128)} %bitcast.7, bf16[48,64,448]{2,1,0:T(8,128)(2,1)} %a_hbm.1, ...), custom_call_target="tpu_custom_call" | custom-call | tf_op jit(solution)/shard_map/pallas_call | solution.py:464
  51.2 0.0 copy-start
  51.2 2.5 %copy.14 = bf16[8,64,1280]{2,1,0:T(8,128)(2,1)} copy(bf16[8,64,1280]{2,1,0:T(8,128)(2,1)} %get-tuple-element.4) | data formatting | bytes 2621440
  53.7 0.0 copy-done
  53.7 0.6 %copy.15 = bf16[8,128]{1,0:T(8,128)(2,1)} copy(bf16[8,128]{1,0:T(8,128)(2,1)S(1)} %copy-done) | data formatting | bytes 4096
Async XLA Ops:
  51.2 2.5 %copy-start = (bf16[8,128]{1,0:T(8,128)(2,1)S(1)}, bf16[8,128]{1,0:T(8,128)(2,1)}, u32[]{:S(2)}) copy-start(bf16[8,128]{1,0:T(8,128)(2,1)} %get-tuple-element.5) | copy-start | bytes 6148

commit v3 on v2

--- a/solution.py
+++ b/solution.py
@@ -34,7 +34,10 @@
     vec_ref,
     own,
     ghost,
-    ghost_send,
+    raw_send,
+    raw_recv,
+    name_send,
+    name_recv,
     rd,
     appl,
     part_send,
@@ -79,7 +82,8 @@
     for copy in inputs:
         copy.start()
 
-    ghost[...] = jnp.zeros_like(ghost)
+    raw_recv[...] = jnp.zeros_like(raw_recv)
+    name_recv[...] = jnp.zeros_like(name_recv)
     part_recv[...] = jnp.zeros_like(part_recv)
     vpart_recv[...] = jnp.zeros_like(vpart_recv)
 
@@ -98,49 +102,74 @@
     pair_lane = lax.broadcasted_iota(jnp.int32, (1, 2 * width), 1)
     first_half = pair_lane < width
 
-    def dense_row(f):
-        strip = p_ref[f]
-        blocks = []
-        for q in range(kp):
-            block = strip[:, q * width : (q + 1) * width]
-            blocks.append(jnp.concatenate([block, block], axis=1))
+    def twice(block):
+        return jnp.concatenate([block, block], axis=1)
+
+    def spread(blocks, names):
         tiles = []
         for s in range(0, nc, 2):
-            here = jnp.where(first_half, s, s + 1)
+            here = jnp.where(first_half, s, s + 1).astype(F32)
             total = None
-            for q in range(kp):
-                term = blocks[q] * jnp.where(here == p_cols[q, f], 1.0, 0.0).astype(BF16)
+            for block, name in zip(blocks, names):
+                term = block * jnp.where(here == name, 1.0, 0.0).astype(BF16)
                 total = term if total is None else total + term
             tiles.append(total)
         return jnp.concatenate(tiles, axis=1)
 
-    def fill_ghosts(listed, at):
+    def dense_row(f):
+        strip = p_ref[f]
+        blocks = [twice(strip[:, q * width : (q + 1) * width]) for q in range(kp)]
+        return spread(blocks, [p_cols[q, f].astype(F32) for q in range(kp)])
+
+    def fill_ghosts(way, listed):
         def body(i, carry):
-            for t in range(UNROLL):
-                g = i * UNROLL + t
-                ghost_send[at + g] = dense_row(listed[g])
+            rows_of = [listed[2 * i], listed[2 * i + 1]]
+            strips = [p_ref[f] for f in rows_of]
+            raw_send[way, i, 0] = strips[0][:, : 2 * width]
+            raw_send[way, i, 1] = strips[1][:, : 2 * width]
+            raw_send[way, i, 2] = jnp.concatenate([x[:, 2 * width :] for x in strips], axis=1)
+            names = [
+                jnp.zeros((1, 2 * width), F32) + p_cols[q, f].astype(F32)
+                for f in rows_of
+                for q in range(kp)
+            ]
+            names.append(jnp.zeros((8 - 2 * kp, 2 * width), F32))
+            name_send[way, i] = jnp.concatenate(names, axis=0)
             return carry
 
-        lax.fori_loop(0, gh // UNROLL, body, 0)
-
-    ghost_up = pltpu.make_async_remote_copy(
-        src_ref=ghost_send.at[pl.ds(0, gh)],
-        dst_ref=ghost.at[pl.ds(0, gh)],
-        send_sem=ghost_sems.at[0],
-        recv_sem=ghost_sems.at[1],
-        device_id=along(1),
-        device_id_type=MESH,
-    )
-    ghost_down = pltpu.make_async_remote_copy(
-        src_ref=ghost_send.at[pl.ds(gh, gh)],
-        dst_ref=ghost.at[pl.ds(gh, gh)],
-        send_sem=ghost_sems.at[2],
-        recv_sem=ghost_sems.at[3],
-        device_id=along(-1),
-        device_id_type=MESH,
-    )
+        lax.fori_loop(0, gh // 2, body, 0)
+
+    def ghost_copies(way):
+        return [
+            pltpu.make_async_remote_copy(
+                src_ref=source.at[way],
+                dst_ref=target.at[way],
+                send_sem=ghost_sems.at[way, i, 0],
+                recv_sem=ghost_sems.at[way, i, 1],
+                device_id=along(2 * way - 1),
+                device_id_type=MESH,
+            )
+            for i, (source, target) in enumerate(((raw_send, raw_recv), (name_send, name_recv)))
+        ]
+
+    def arrived_ghosts(way, at):
+        def body(i, carry):
+            last = raw_recv[way, i, 2]
+            for t in range(2):
+                pair = raw_recv[way, i, t]
+                blocks = [
+                    twice(pair[:, :width]),
+                    twice(pair[:, width:]),
+                    twice(last[:, t * width : (t + 1) * width]),
+                ]
+                names = [name_recv[way, i, t * kp + q : t * kp + q + 1, :] for q in range(kp)]
+                ghost[at + 2 * i + t] = spread(blocks, names)
+            return carry
+
+        lax.fori_loop(0, gh // 2, body, 0)
+
     inputs[0].wait()
-    fill_ghosts(up_rows, 0)
+    fill_ghosts(1, up_rows)
     pl.semaphore_wait(
         barrier,
         comp_count - 1 + jnp.where(has_below, 1, 0) + jnp.where(has_above, 1, 0),
@@ -148,13 +177,15 @@
 
     @pl.when(has_above)
     def _():
-        ghost_up.start()
-
-    fill_ghosts(down_rows, gh)
+        for copy in ghost_copies(1):
+            copy.start()
+
+    fill_ghosts(0, down_rows)
 
     @pl.when(has_below)
     def _():
-        ghost_down.start()
+        for copy in ghost_copies(0):
+            copy.start()
 
     def own_body(i, carry):
         for t in range(UNROLL):
@@ -194,6 +225,76 @@
 
     lax.fori_loop(0, nf // 2, rd_body, 0)
 
+    def vpart_copy(way):
+        return pltpu.make_async_remote_copy(
+            src_ref=vpart_send.at[way],
+            dst_ref=vpart_recv.at[way],
+            send_sem=vpart_sems.at[way, 0],
+            recv_sem=vpart_sems.at[way, 1],
+            device_id=along(2 * way - 1),
+            device_id_type=MESH,
+        )
+
+    def part_copy(way, e):
+        return pltpu.make_async_remote_copy(
+            src_ref=part_send.at[way, e],
+            dst_ref=part_recv.at[way, e],
+            send_sem=part_sems.at[way, e, 0],
+            recv_sem=part_sems.at[way, e, 1],
+            device_id=along(2 * way - 1),
+            device_id_type=MESH,
+        )
+
+    sends_to = (has_below, has_above)
+    gets_from = (has_above, has_below)
+
+    def start(copy, way):
+        @pl.when(sends_to[way])
+        def _():
+            copy.start()
+
+    def wait_recv(copy, way):
+        @pl.when(gets_from[way])
+        def _():
+            copy.wait_recv()
+
+    def wait_send(copy, way):
+        @pl.when(sends_to[way])
+        def _():
+            copy.wait_send()
+
+    a_lane = lax.broadcasted_iota(jnp.int32, (1, ka * width), 1)
+
+    def columns_of(f):
+        cols = [a_cols[k, f] for k in range(ka)]
+        row = jnp.where(a_lane < width, cols[0], cols[1])
+        for k in range(2, ka):
+            row = jnp.where(a_lane >= k * width, cols[k], row)
+        return cols, row
+
+    def at_row(f):
+        return pl.ds(pl.multiple_of(f * width, width), width)
+
+    def near_body(i, carry):
+        for t in range(WIDE):
+            f = i * WIDE + t
+            cols, row = columns_of(f)
+            keep = jnp.where(row < nf, 1.0, 0.0).astype(BF16)
+            table = jnp.concatenate([own[jnp.where(x < nf, x, 0)] for x in cols], axis=0)
+            product = jnp.dot(a_ref[f] * keep, table, preferred_element_type=F32)
+            appl[1, at_row(f), :] = product.astype(BF16)
+        return carry
+
+    inputs[3].wait()
+    lax.fori_loop(0, nf // WIDE, near_body, 0)
+
+    def restrict(e):
+        terms = jnp.dot(rd[...], appl[e], preferred_element_type=F32)
+        part_send[0, e] = terms[:seg].astype(BF16)
+        own_part[e] = terms[seg : 2 * seg]
+        part_send[1, e] = terms[2 * seg :].astype(BF16)
+
+    restrict(1)
     vec_part = lax.dot_general(
         vec_t[...].astype(BF16),
         rd[...],
@@ -203,90 +304,22 @@
     vpart_send[0] = vec_part[:, 0:seg]
     vpart_send[1] = vec_part[:, 2 * seg : 3 * seg]
     vec_own = vec_part[:, seg : 2 * seg]
-
-    def vpart_copy(way):
-        return pltpu.make_async_remote_copy(
-            src_ref=vpart_send.at[way],
-            dst_ref=vpart_recv.at[way],
-            send_sem=vpart_sems.at[way, 0],
-            recv_sem=vpart_sems.at[way, 1],
-            device_id=along(2 * way - 1),
-            device_id_type=MESH,
-        )
-
-    def part_copy(way, e):
-        return pltpu.make_async_remote_copy(
-            src_ref=part_send.at[way, e],
-            dst_ref=part_recv.at[way, e],
-            send_sem=part_sems.at[way, e, 0],
-            recv_sem=part_sems.at[way, e, 1],
-            device_id=along(2 * way - 1),
-            device_id_type=MESH,
-        )
-
-    sends_to = (has_below, has_above)
-    gets_from = (has_above, has_below)
-
-    def start(copy, way):
-        @pl.when(sends_to[way])
-        def _():
-            copy.start()
-
-    def wait_recv(copy, way):
-        @pl.when(gets_from[way])
-        def _():
+    @pl.when(has_below)
+    def _():
+        for copy in ghost_copies(1):
             copy.wait_recv()
 
-    def wait_send(copy, way):
-        @pl.when(sends_to[way])
-        def _():
-            copy.wait_send()
-
+    @pl.when(has_above)
+    def _():
+        for copy in ghost_copies(0):
+            copy.wait_recv()
+
+    for way in range(2):
+        start(part_copy(way, 1), way)
     for way in range(2):
         start(vpart_copy(way), way)
-
-    a_lane = lax.broadcasted_iota(jnp.int32, (1, ka * width), 1)
-
-    def columns_of(f):
-        cols = [a_cols[k, f] for k in range(ka)]
-        row = jnp.where(a_lane < width, cols[0], cols[1])
-        for k in range(2, ka):
-            row = jnp.where(a_lane >= k * width, cols[k], row)
-        return cols, row
-
-    def at_row(f):
-        return pl.ds(pl.multiple_of(f * width, width), width)
-
-    def near_body(i, carry):
-        for t in range(WIDE):
-            f = i * WIDE + t
-            cols, row = columns_of(f)
-            keep = jnp.where(row < nf, 1.0, 0.0).astype(BF16)
-            table = jnp.concatenate([own[jnp.where(x < nf, x, 0)] for x in cols], axis=0)
-            product = jnp.dot(a_ref[f] * keep, table, preferred_element_type=F32)
-            appl[1, at_row(f), :] = product.astype(BF16)
-        return carry
-
-    inputs[3].wait()
-    lax.fori_loop(0, nf // WIDE, near_body, 0)
-
-    def restrict(e):
-        terms = jnp.dot(rd[...], appl[e], preferred_element_type=F32)
-        part_send[0, e] = terms[:seg].astype(BF16)
-        own_part[e] = terms[seg : 2 * seg]
-        part_send[1, e] = terms[2 * seg :].astype(BF16)
-
-    restrict(1)
-    for way in range(2):
-        start(part_copy(way, 1), way)
-
-    @pl.when(has_below)
-    def _():
-        ghost_up.wait_recv()
-
-    @pl.when(has_above)
-    def _():
-        ghost_down.wait_recv()
+    arrived_ghosts(1, 0)
+    arrived_ghosts(0, gh)
 
     def far_body(i, carry):
         for t in range(WIDE):
@@ -431,11 +464,13 @@
 
     @pl.when(has_above)
     def _():
-        ghost_up.wait_send()
+        for copy in ghost_copies(1):
+            copy.wait_send()
 
     @pl.when(has_below)
     def _():
-        ghost_down.wait_send()
+        for copy in ghost_copies(0):
+            copy.wait_send()
 
 
 def on_device(
@@ -476,7 +511,10 @@
             pltpu.VMEM(vectors.shape, BF16),
             pltpu.VMEM((nf, width, seg), BF16),
             pltpu.VMEM((2 * gh, width, seg), BF16),
-            pltpu.VMEM((2 * gh, width, seg), BF16),
+            pltpu.VMEM((2, gh // 2, kp, width, 2 * width), BF16),
+            pltpu.VMEM((2, gh // 2, kp, width, 2 * width), BF16),
+            pltpu.VMEM((2, gh // 2, 8, 2 * width), F32),
+            pltpu.VMEM((2, gh // 2, 8, 2 * width), F32),
             pltpu.VMEM((3 * seg, nf * width), BF16),
             pltpu.VMEM((3, nf * width, seg), BF16),
             pltpu.VMEM((2, 3, seg, seg), BF16),
@@ -491,7 +529,7 @@
             pltpu.VMEM((nc + 1, 8, 2 * width), F32),
             pltpu.VMEM((comp_count, cap, 8, 2 * width), F32),
             pltpu.VMEM((comp_count, cap, 8, 2 * width), F32),
-            pltpu.SemaphoreType.DMA((4,)),
+            pltpu.SemaphoreType.DMA((2, 2, 2)),
             pltpu.SemaphoreType.DMA((2, 3, 2)),
             pltpu.SemaphoreType.DMA((2, 2)),
             pltpu.SemaphoreType.DMA((5, comp_count - 1, 2)),

time: 54.5 us -> 49.5 us (0.908)
  Pallas kernels: 50.6 us -> 45.7 us
    pallas_call x1, Pallas kernels: 50.6 us -> 45.7 us  [on_device(): pl.pallas_call(functools.partial(kernel, sizes), out_shape=(jax.ShapeDtyp...]
where the time goes in v3:
time: 49.5 us; the launch traced here: 49.4 us
  Pallas kernels  45.7 us (92%)
  local copies, waits for them, and re-layouts  3.05 us (6%)
  between operations  0.65 us (1%)
    pallas_call x1, Pallas kernels, on_device(): pl.pallas_call(functools.partial(kernel, sizes), out_shape=(jax.ShapeDtyp...  45.7 us
    unnamed x4, local copies, waits for them, and re-layouts  3.05 us

profile of v3, /device:TPU:9, one launch (start us, length us, event | category | flops | bytes accessed | tf_op | source)
XLA Modules:
  0.0 49.4 jit_solution(7894593813124136108)
XLA Ops:
  0.6 45.7 %shard_map.113 = (bf16[8,64,1280]{2,1,0:T(8,128)(2,1)}, bf16[8,128]{1,0:T(8,128)(2,1)}) custom-call(s32[7,48]{1,0:T(8,128)} %bitcast.4, s32[3,48]{1,0:T(4,128)} %bitcast.5, s32[3,48]{1,0:T(4,128)} %bitcast.6, s32[12]{0:T(128)} %up_rows.1, s32[12]{0:T(128)} %down_rows.1, s32[4]{0:T(128)} %bitcast.7, bf16[48,64,448]{2,1,0:T(8,128)(2,1)} %a_hbm.1, ...), custom_call_target="tpu_custom_call" | custom-call | tf_op jit(solution)/shard_map/pallas_call | solution.py:499
  46.3 0.0 copy-start
  46.3 2.5 %copy.14 = bf16[8,64,1280]{2,1,0:T(8,128)(2,1)} copy(bf16[8,64,1280]{2,1,0:T(8,128)(2,1)} %get-tuple-element.4) | data formatting | bytes 2621440
  48.8 0.0 copy-done
  48.8 0.6 %copy.15 = bf16[8,128]{1,0:T(8,128)(2,1)} copy(bf16[8,128]{1,0:T(8,128)(2,1)S(1)} %copy-done) | data formatting | bytes 4096
Async XLA Ops:
  46.3 2.5 %copy-start = (bf16[8,128]{1,0:T(8,128)(2,1)S(1)}, bf16[8,128]{1,0:T(8,128)(2,1)}, u32[]{:S(2)}) copy-start(bf16[8,128]{1,0:T(8,128)(2,1)} %get-tuple-element.5) | copy-start | bytes 6148

commit v4 on v3

--- a/solution.py
+++ b/solution.py
@@ -235,12 +235,17 @@
             device_id_type=MESH,
         )
 
-    def part_copy(way, e):
+    half = seg // 2
+
+    def part_copy(way, e, upper=False):
+        last = e == 2 * way
+        lanes = pl.ds(half if upper else 0, half if last else seg)
+        at = 3 if upper else e
         return pltpu.make_async_remote_copy(
-            src_ref=part_send.at[way, e],
-            dst_ref=part_recv.at[way, e],
-            send_sem=part_sems.at[way, e, 0],
-            recv_sem=part_sems.at[way, e, 1],
+            src_ref=part_send.at[way, e, :, lanes],
+            dst_ref=part_recv.at[way, e, :, lanes],
+            send_sem=part_sems.at[way, at, 0],
+            recv_sem=part_sems.at[way, at, 1],
             device_id=along(2 * way - 1),
             device_id_type=MESH,
         )
@@ -340,8 +345,9 @@
     start(part_copy(1, 0), 1)
     restrict(2)
     start(part_copy(0, 2), 0)
-    start(part_copy(1, 2), 1)
-    start(part_copy(0, 0), 0)
+    for upper in (False, True):
+        start(part_copy(1, 2, upper), 1)
+        start(part_copy(0, 0, upper), 0)
 
     owners = [dest[s] for s in range(nc)]
     ranks = []
@@ -361,42 +367,50 @@
 
     own_rows = pl.ds(c * cap, cap)
 
-    def slot_copy(u, r):
+    pieces = [(0, 0, seg), (1, 0, seg), (2, 0, half), (3, 0, seg), (4, 0, seg), (2, half, half)]
+
+    def slot_copy(piece, r):
+        u, low, count = pieces[piece]
         return pltpu.make_async_remote_copy(
-            src_ref=slots.at[u, r],
-            dst_ref=out_ref.at[own_rows, :, pl.ds(u * seg, seg)],
-            send_sem=slot_sems.at[u, r - 1, 0],
-            recv_sem=slot_sems.at[u, r - 1, 1],
+            src_ref=slots.at[u, r, :, :, pl.ds(low, count)],
+            dst_ref=out_ref.at[own_rows, :, pl.ds(u * seg + low, count)],
+            send_sem=slot_sems.at[piece, r - 1, 0],
+            recv_sem=slot_sems.at[piece, r - 1, 1],
             device_id=peer(r),
             device_id_type=MESH,
         )
 
-    def local_copy(u):
+    def local_copy(piece):
+        u, low, count = pieces[piece]
         return pltpu.make_async_copy(
-            slots.at[u, 0], out_ref.at[own_rows, :, pl.ds(u * seg, seg)], local_sems.at[u]
+            slots.at[u, 0, :, :, pl.ds(low, count)],
+            out_ref.at[own_rows, :, pl.ds(u * seg + low, count)],
+            local_sems.at[piece],
         )
 
-    def finish(u):
+    def finish(piece):
+        u, low, count = pieces[piece]
+        cut = slice(low, low + count)
         total = None
         if 1 <= u <= 3:
-            total = own_part[u - 1]
+            total = own_part[u - 1, :, cut]
         if u >= 2:
-            term = part_recv[0, u - 2].astype(F32)
+            term = part_recv[0, u - 2, :, cut].astype(F32)
             total = term if total is None else total + term
         if u <= 2:
-            term = part_recv[1, u].astype(F32)
+            term = part_recv[1, u, :, cut].astype(F32)
             total = term if total is None else total + term
         rounded = total.astype(BF16)
         for s in range(nc):
-            rows[u, s] = rounded[s * width : (s + 1) * width]
-        rows[u, nc] = jnp.zeros((width, seg), BF16)
+            rows[u, s, :, cut] = rounded[s * width : (s + 1) * width]
+        rows[u, nc, :, cut] = jnp.zeros((width, count), BF16)
         for r in range(1, comp_count):
             for k in range(cap):
-                slots[u, r, k] = rows[u, sources[r * cap + k]]
-            slot_copy(u, r).start()
+                slots[u, r, k, :, cut] = rows[u, sources[r * cap + k], :, cut]
+            slot_copy(piece, r).start()
         for k in range(cap):
-            slots[u, 0, k] = rows[u, sources[k]]
-        local_copy(u).start()
+            slots[u, 0, k, :, cut] = rows[u, sources[k], :, cut]
+        local_copy(piece).start()
 
     for way in range(2):
         wait_recv(vpart_copy(way), way)
@@ -435,6 +449,9 @@
     wait_recv(part_copy(1, 2), 1)
     wait_recv(part_copy(0, 0), 0)
     finish(2)
+    wait_recv(part_copy(1, 2, True), 1)
+    wait_recv(part_copy(0, 0, True), 0)
+    finish(5)
 
     vslots_recv[0] = vslots[0]
     for r in range(1, comp_count):
@@ -449,18 +466,19 @@
             vec_rows.append(row)
     out_vec[...] = jnp.concatenate(vec_rows, axis=0).astype(BF16)
 
-    for u in range(5):
+    for piece in range(len(pieces)):
         for r in range(1, comp_count):
-            slot_copy(u, r).wait_recv()
-        local_copy(u).wait()
+            slot_copy(piece, r).wait_recv()
+        local_copy(piece).wait()
     for r in range(1, comp_count):
         vslot_copy(r).wait_send()
-        for u in range(5):
-            slot_copy(u, r).wait_send()
+        for piece in range(len(pieces)):
+            slot_copy(piece, r).wait_send()
     for way in range(2):
         wait_send(vpart_copy(way), way)
         for e in range(3):
             wait_send(part_copy(way, e), way)
+        wait_send(part_copy(way, 2 * way, True), way)
 
     @pl.when(has_above)
     def _():
@@ -471,6 +489,21 @@
     def _():
         for copy in ghost_copies(0):
             copy.wait_send()
+
+
+def hand_on(matrix_in, vecs_in, matrix, vecs, sems):
+    count = matrix_in.shape[0] // 2
+    copies = [
+        pltpu.make_async_copy(
+            matrix_in.at[pl.ds(2 * i, 2)], matrix.at[pl.ds(2 * i, 2)], sems.at[i]
+        )
+        for i in range(count)
+    ]
+    copies.append(pltpu.make_async_copy(vecs_in, vecs, sems.at[count]))
+    for copy in copies:
+        copy.start()
+    for copy in copies:
+        copy.wait()
 
 
 def on_device(
@@ -496,12 +529,13 @@
     smem = pl.BlockSpec(memory_space=pltpu.SMEM)
     hbm = pl.BlockSpec(memory_space=pl.ANY)
     vmem = pl.BlockSpec(memory_space=pltpu.VMEM)
-    return pl.pallas_call(
+    shapes = (
+        jax.ShapeDtypeStruct((comp_count * cap, width, 5 * seg), BF16),
+        jax.ShapeDtypeStruct((comp_count * cap, 2 * width), BF16),
+    )
+    found = pl.pallas_call(
         functools.partial(kernel, sizes),
-        out_shape=(
-            jax.ShapeDtypeStruct((comp_count * cap, width, 5 * seg), BF16),
-            jax.ShapeDtypeStruct((comp_count * cap, 2 * width), BF16),
-        ),
+        out_shape=shapes,
         in_specs=[smem] * 6 + [hbm] * 4,
         out_specs=(hbm, vmem),
         scratch_shapes=[
@@ -530,10 +564,10 @@
             pltpu.VMEM((comp_count, cap, 8, 2 * width), F32),
             pltpu.VMEM((comp_count, cap, 8, 2 * width), F32),
             pltpu.SemaphoreType.DMA((2, 2, 2)),
-            pltpu.SemaphoreType.DMA((2, 3, 2)),
+            pltpu.SemaphoreType.DMA((2, 4, 2)),
             pltpu.SemaphoreType.DMA((2, 2)),
-            pltpu.SemaphoreType.DMA((5, comp_count - 1, 2)),
-            pltpu.SemaphoreType.DMA((5,)),
+            pltpu.SemaphoreType.DMA((6, comp_count - 1, 2)),
+            pltpu.SemaphoreType.DMA((6,)),
             pltpu.SemaphoreType.DMA((comp_count - 1, 2)),
             pltpu.SemaphoreType.DMA((4,)),
         ],
@@ -552,6 +586,14 @@
         r_blocks,
         vectors,
     )
+    return pl.pallas_call(
+        hand_on,
+        out_shape=shapes,
+        in_specs=[hbm, hbm],
+        out_specs=(hbm, hbm),
+        scratch_shapes=[pltpu.SemaphoreType.DMA((comp_count * cap // 2 + 1,))],
+        compiler_params=pltpu.CompilerParams(vmem_limit_bytes=60 * 1024 * 1024),
+    )(*found)
 
 
 def solution(mesh):

time: 49.5 us -> 87.5 us (1.77)
  Pallas kernels: 45.7 us -> 86.7 us
  local copies, waits for them, and re-layouts: 3.05 us -> 0 us
    pallas_call x1 -> x2, Pallas kernels: 45.7 us -> 86.7 us  [the longest x1 45.8 us: on_device(): pl.pallas_call(functools.partial(kernel, sizes), out_shape=shapes, in_spe...]
    unnamed x4 -> x0, local copies, waits for them, and re-layouts: 3.05 us -> none
where the time goes in v4:
time: 87.5 us; the launch traced here: 87.3 us
  Pallas kernels  86.7 us (99%)
    pallas_call x1, Pallas kernels, on_device(): pl.pallas_call(functools.partial(kernel, sizes), out_shape=shapes, in_spe...  45.8 us
    pallas_call x1, Pallas kernels, on_device(): pl.pallas_call(hand_on, out_shape=shapes, in_specs=[hbm, hbm], out_specs=...  40.9 us

profile of v4, /device:TPU:9, one launch (start us, length us, event | category | flops | bytes accessed | tf_op | source)
XLA Modules:
  0.0 87.3 jit_solution(13168834482667125096)
XLA Ops:
  0.6 45.8 %shard_map.113 = (bf16[8,64,1280]{2,1,0:T(8,128)(2,1)}, bf16[8,128]{1,0:T(8,128)(2,1)}) custom-call(s32[7,48]{1,0:T(8,128)} %bitcast.4, s32[3,48]{1,0:T(4,128)} %bitcast.5, s32[3,48]{1,0:T(4,128)} %bitcast.6, s32[12]{0:T(128)} %up_rows.1, s32[12]{0:T(128)} %down_rows.1, s32[4]{0:T(128)} %bitcast.7, bf16[48,64,448]{2,1,0:T(8,128)(2,1)} %a_hbm.1, ...), custom_call_target="tpu_custom_call" | custom-call | tf_op jit(solution)/shard_map/pallas_call | solution.py:536
  46.4 40.9 %shard_map.114 = (bf16[8,64,1280]{2,1,0:T(8,128)(2,1)}, bf16[8,128]{1,0:T(8,128)(2,1)}) custom-call(bf16[8,64,1280]{2,1,0:T(8,128)(2,1)} %get-tuple-element.4.matrix_in, bf16[8,128]{1,0:T(8,128)(2,1)} %get-tuple-element.5.vecs_in), custom_call_target="tpu_custom_call" | custom-call | tf_op jit(solution)/shard_map/pallas_call | solution.py:589

commit v5 on v3

--- a/solution.py
+++ b/solution.py
@@ -473,6 +473,23 @@
             copy.wait_send()
 
 
+def hand_on(matrix_in, vecs_in, matrix, vecs, held, held_vecs, sems):
+    count = held.shape[0] // 2
+    loads = [pltpu.make_async_copy(vecs_in, held_vecs, sems.at[0, count])]
+    stores = [pltpu.make_async_copy(held_vecs, vecs, sems.at[1, count])]
+    for i in range(count):
+        part = pl.ds(2 * i, 2)
+        loads.append(pltpu.make_async_copy(matrix_in.at[part], held.at[part], sems.at[0, i]))
+        stores.append(pltpu.make_async_copy(held.at[part], matrix.at[part], sems.at[1, i]))
+    for load in loads:
+        load.start()
+    for load, store in zip(loads, stores):
+        load.wait()
+        store.start()
+    for store in stores:
+        store.wait()
+
+
 def on_device(
     mesh_count,
     comp_count,
@@ -496,12 +513,13 @@
     smem = pl.BlockSpec(memory_space=pltpu.SMEM)
     hbm = pl.BlockSpec(memory_space=pl.ANY)
     vmem = pl.BlockSpec(memory_space=pltpu.VMEM)
-    return pl.pallas_call(
+    shapes = (
+        jax.ShapeDtypeStruct((comp_count * cap, width, 5 * seg), BF16),
+        jax.ShapeDtypeStruct((comp_count * cap, 2 * width), BF16),
+    )
+    found = pl.pallas_call(
         functools.partial(kernel, sizes),
-        out_shape=(
-            jax.ShapeDtypeStruct((comp_count * cap, width, 5 * seg), BF16),
-            jax.ShapeDtypeStruct((comp_count * cap, 2 * width), BF16),
-        ),
+        out_shape=shapes,
         in_specs=[smem] * 6 + [hbm] * 4,
         out_specs=(hbm, vmem),
         scratch_shapes=[
@@ -552,6 +570,18 @@
         r_blocks,
         vectors,
     )
+    return pl.pallas_call(
+        hand_on,
+        out_shape=shapes,
+        in_specs=[hbm, hbm],
+        out_specs=(hbm, hbm),
+        scratch_shapes=[
+            pltpu.VMEM(shapes[0].shape, BF16),
+            pltpu.VMEM(shapes[1].shape, BF16),
+            pltpu.SemaphoreType.DMA((2, comp_count * cap // 2 + 1)),
+        ],
+        compiler_params=pltpu.CompilerParams(vmem_limit_bytes=60 * 1024 * 1024),
+    )(*found)
 
 
 def solution(mesh):

time: 49.5 us -> 48.6 us (0.982)
  local copies, waits for them, and re-layouts: 3.05 us -> 0 us
  Pallas kernels: 45.7 us -> 47.8 us
    unnamed x4 -> x0, local copies, waits for them, and re-layouts: 3.05 us -> none
    pallas_call x1 -> x2, Pallas kernels: 45.7 us -> 47.8 us  [the longest x1 45.7 us: on_device(): pl.pallas_call(functools.partial(kernel, sizes), out_shape=shapes, in_spe...]
where the time goes in v5:
time: 48.6 us; the launch traced here: 48.4 us
  Pallas kernels  47.8 us (98%)
  between operations  0.64 us (1%)
    pallas_call x1, Pallas kernels, on_device(): pl.pallas_call(functools.partial(kernel, sizes), out_shape=shapes, in_spe...  45.7 us
    pallas_call x1, Pallas kernels, on_device(): pl.pallas_call(hand_on, out_shape=shapes, in_specs=[hbm, hbm], out_specs=...  2.11 us

profile of v5, /device:TPU:9, one launch (start us, length us, event | category | flops | bytes accessed | tf_op | source)
XLA Modules:
  0.0 48.4 jit_solution(1550832798999253141)
XLA Ops:
  0.6 45.7 %shard_map.113 = (bf16[8,64,1280]{2,1,0:T(8,128)(2,1)}, bf16[8,128]{1,0:T(8,128)(2,1)}) custom-call(s32[7,48]{1,0:T(8,128)} %bitcast.4, s32[3,48]{1,0:T(4,128)} %bitcast.5, s32[3,48]{1,0:T(4,128)} %bitcast.6, s32[12]{0:T(128)} %up_rows.1, s32[12]{0:T(128)} %down_rows.1, s32[4]{0:T(128)} %bitcast.7, bf16[48,64,448]{2,1,0:T(8,128)(2,1)} %a_hbm.1, ...), custom_call_target="tpu_custom_call" | custom-call | tf_op jit(solution)/shard_map/pallas_call | solution.py:520
  46.3 2.1 %shard_map.114 = (bf16[8,64,1280]{2,1,0:T(8,128)(2,1)}, bf16[8,128]{1,0:T(8,128)(2,1)}) custom-call(bf16[8,64,1280]{2,1,0:T(8,128)(2,1)} %get-tuple-element.4.matrix_in, bf16[8,128]{1,0:T(8,128)(2,1)} %get-tuple-element.5.vecs_in), custom_call_target="tpu_custom_call" | custom-call | tf_op jit(solution)/shard_map/pallas_call | solution.py:573
